TPU v7x, 32 devices: a whole 2x2x4 slice. The times are simulated.
32 devices in a mesh: dp: 4 (over y, x), expert: 8 (over z, core).
Axes of the slice: x: 2, y: 2, z: 4, core: 2. Of those that a mesh axis runs over, the one named last changes fastest.
Arguments:
- slot_grads: bfloat16 [4, 8, 384, 2048], P('dp', 'expert'), may hold values from -0.23925781 to 0.23925781
- momentum: float32 [384, 4, 2048], P('expert', None, 'dp'), may hold values from -0.16 to 0.16
- master_weights: float32 [384, 4, 2048], P('expert', None, 'dp'), may hold values from -0.3125 to 0.3125
- current_slots: int32 [8, 1], replicated, may hold values from 0 to 3
- next_slots: int32 [8, 1], replicated, may hold values from 0 to 3
- live_counts: int32 [4, 8], P('dp', 'expert'), may hold values from 1 to 512
- route_index: int32 [4, 8, 4, 128], P('dp', 'expert'), may hold values from 0 to 127, each once within a row
- activations: bfloat16 [4, 8, 512, 384], P('dp', 'expert'), may hold values from -6 to 6
Outputs:
- new_momentum: float32 [384, 4, 2048], P('expert', None, 'dp')
- expert_out: bfloat16 [4, 8, 512, 2048], P('dp', 'expert')
Inputs may be any that keep to these rules, and one draw needn't show every extreme that they name: `current_slots`: every expert is held by at least one slot. `next_slots`: every expert is held by at least one slot. `route_index`: each block of 128 indices names every row of its block once.
All inputs are finite; a program needn't handle non-finite values.
Results may differ from a plain program's by a relative error of at most 0.015.
Values may be sent and summed in bfloat16 or wider, within the bound.
No kernel may reach another device: no remote copies, remote signals or barrier semaphores. Data moves between devices by JAX's collectives and lax.ppermute only.
A program may use at most 64 MiB of HBM per device.

v0:
```python
import jax
import jax.numpy as jnp
from jax import lax
from jax.sharding import PartitionSpec as P

QBLOCK = 128


momentum_decay = 0.9
step_rate = 0.5
epsilon = 1e-06
range_limit = 448.0


def select_rows(activations, route_index):
    block_count = route_index.shape[2]
    block_rows = route_index.shape[3]
    hidden_rows = activations.shape[3]
    blocked = activations[0, 0].reshape(block_count, block_rows, hidden_rows)
    picked = jnp.take_along_axis(blocked, route_index[0, 0][:, :, None], axis=1)
    return picked.reshape(block_count * block_rows, hidden_rows)


def dequantize(values, scales):
    hidden_rows, columns = values.shape
    expanded = values.reshape(hidden_rows, columns // QBLOCK, QBLOCK).astype(jnp.float32)
    expanded = expanded * scales.astype(jnp.float32)[:, :, None]
    return expanded.reshape(hidden_rows, columns).astype(jnp.bfloat16)


def shards(
    slot_grads,
    momentum,
    master_weights,
    current_slots,
    next_slots,
    live_counts,
    route_index,
    activations,
):
    expert_count = lax.axis_size("expert")
    gradient = slot_grads[0, 0]
    hidden_rows = gradient.shape[0]
    slice_rows = hidden_rows // expert_count
    experts = momentum.shape[1]
    columns = momentum.shape[2]
    labels = jnp.arange(experts, dtype=jnp.int32)
    owner_table = current_slots[:, 0][None, :] == labels[:, None]
    summed = lax.psum_scatter(
        gradient.astype(jnp.float32).astype(jnp.bfloat16), "dp", scatter_dimension=1, tiled=True
    ).astype(jnp.float32)
    pieces = summed.reshape(expert_count, slice_rows, columns)
    received = lax.all_to_all(
        pieces.astype(jnp.bfloat16), "expert", split_axis=0, concat_axis=0, tiled=True
    ).astype(pieces.dtype)
    totals = jnp.einsum(
        "xs,spk->pxk", owner_table.astype(jnp.float32), received, precision=lax.Precision.HIGHEST
    )
    new_momentum = momentum_decay * momentum + totals
    weights = master_weights - step_rate * new_momentum
    blocks = weights.reshape(slice_rows, experts, columns // QBLOCK, QBLOCK)
    previous = master_weights.reshape(slice_rows, experts, columns // QBLOCK, QBLOCK)
    scales = (jnp.max(jnp.abs(previous), axis=3) / range_limit + epsilon).astype(jnp.bfloat16)
    scaled = blocks / scales.astype(jnp.float32)[:, :, :, None]
    quantized = jnp.clip(scaled, -range_limit, range_limit).astype(jnp.bfloat16)
    quantized = quantized.reshape(slice_rows, experts, columns)
    chooser = (next_slots[:, 0][:, None] == labels[None, :]).astype(jnp.bfloat16)
    selected = select_rows(activations, route_index)
    sent_values = jnp.einsum(
        "sx,pxk->spk", chooser, quantized, preferred_element_type=jnp.float32
    ).astype(jnp.bfloat16)
    sent_scales = jnp.einsum(
        "sx,pxb->spb", chooser, scales, preferred_element_type=jnp.float32
    ).astype(jnp.bfloat16)
    got_values, got_scales = (
        lax.all_to_all(sent_values, "expert", split_axis=0, concat_axis=0, tiled=True),
        lax.all_to_all(sent_scales, "expert", split_axis=0, concat_axis=0, tiled=True),
    )
    weight_cols = dequantize(
        got_values.reshape(hidden_rows, columns), got_scales.reshape(hidden_rows, columns // QBLOCK)
    )
    product = jnp.dot(
        selected,
        lax.all_gather(weight_cols, "dp", axis=1, tiled=True),
        preferred_element_type=jnp.float32,
    )
    live = jnp.arange(product.shape[0], dtype=jnp.int32) < live_counts[0, 0]
    expert_out = jnp.where(live[:, None], product, 0.0).astype(jnp.bfloat16)
    return (new_momentum, expert_out[None, None])


def solution(mesh):
    in_specs = (
        P("dp", "expert", None, None),
        P("expert", None, "dp"),
        P("expert", None, "dp"),
        P(),
        P(),
        P("dp", "expert"),
        P("dp", "expert", None, None),
        P("dp", "expert", None, None),
    )
    out_specs = (P("expert", None, "dp"), P("dp", "expert", None, None))
    return jax.shard_map(shards, mesh=mesh, in_specs=in_specs, out_specs=out_specs, check_vma=False)
```

profile of v0, /device:TPU:0, one launch (start us, length us, event | category | flops | bytes accessed | tf_op | source)
XLA Modules:
  0.0 127.9 jit_solution(16480999453433087713)
XLA Ops:
  7.2 0.0 copy-start
  7.2 0.0 copy-start.1
  7.2 0.0 reduce-scatter.2.cloned.1.call-start
  7.2 0.0 copy-start.6
  7.2 0.7 reduce-scatter.2.cloned.1.call-update
  7.9 36.7 %reduce-scatter.2.cloned.1.call-done = bf16[384,512]{1,0:T(8,128)(2,1)} async-done(((bf16[384,2048]{1,0:T(8,128)(2,1)}), bf16[384,512]{1,0:T(8,128)(2,1)}) %reduce-scatter.2.cloned.1.call-update) | async-done | bytes 393232 | tf_op jit(solution)/shard_map/reduce_scatter | solution.py:49
  44.7 0.0 copy-start.2
  44.7 0.0 copy-start.5
  44.7 4.7 %all-to-all-start = ((bf16[8,48,512]{2,1,0:T(8,128)(2,1)}), bf16[8,48,512]{2,1,0:T(8,128)(2,1)S(1)}, u32[]{:S(2)}, u32[]{:S(2)}) async-start(bf16[8,48,512]{2,1,0:T(8,128)(2,1)} %bitcast.42), calls=%async_computation.1 | async-start | bytes 786432 | tf_op jit(solution)/shard_map/all_to_all | solution.py:53
  49.4 0.0 copy-done.1
  49.4 0.1 abs.6
  49.5 0.2 abs.7
  49.7 0.4 reduce_max.9
  50.1 0.1 copy.27
  50.2 0.1 copy.28
  50.4 0.0 copy-done.6
  50.4 0.2 convolution_convert_fusion.1
  50.6 0.6 copy.31
  51.2 0.3 div.19
  51.4 0.2 div.20
  51.7 10.3 %all-to-all-done = bf16[8,48,512]{2,1,0:T(8,128)(2,1)S(1)} async-done(((bf16[8,48,512]{2,1,0:T(8,128)(2,1)}), bf16[8,48,512]{2,1,0:T(8,128)(2,1)S(1)}, u32[]{:S(2)}, u32[]{:S(2)}) %all-to-all-start) | async-done | bytes 393248 | tf_op jit(solution)/shard_map/all_to_all | solution.py:53
  62.0 3.3 %all-to-all-start.2 = ((bf16[8,48,4]{1,2,0:T(4,128)(2,1)}), bf16[8,48,4]{1,2,0:T(4,128)(2,1)S(1)}, u32[]{:S(2)}, u32[]{:S(2)}) async-start(bf16[8,48,4]{1,2,0:T(4,128)(2,1)} %copy.31), calls=%async_computation.3 | async-start | bytes 16384 | tf_op jit(solution)/shard_map/all_to_all | solution.py:77
  65.3 0.0 copy-done.2
  65.3 0.0 copy-done.5
  65.3 0.3 fusion.1
  65.6 0.0 copy-start.3
  65.7 0.3 convolution_convert_fusion
  66.0 0.9 copy.29
  66.8 0.0 copy-start.4
  66.8 4.0 %all-to-all-done.2 = bf16[8,48,4]{1,2,0:T(4,128)(2,1)S(1)} async-done(((bf16[8,48,4]{1,2,0:T(4,128)(2,1)}), bf16[8,48,4]{1,2,0:T(4,128)(2,1)S(1)}, u32[]{:S(2)}, u32[]{:S(2)}) %all-to-all-start.2) | async-done | bytes 3104 | tf_op jit(solution)/shard_map/all_to_all | solution.py:77
  70.8 0.0 copy-done.3
  70.8 3.5 %all-to-all-start.1 = ((bf16[8,48,512]{2,1,0:T(8,128)(2,1)}), bf16[8,48,512]{2,1,0:T(8,128)(2,1)S(1)}, u32[]{:S(2)}, u32[]{:S(2)}) async-start(bf16[8,48,512]{2,1,0:T(8,128)(2,1)} %copy.29), calls=%async_computation.2 | async-start | bytes 786432 | tf_op jit(solution)/shard_map/all_to_all | solution.py:76
  74.3 0.0 all-gather.2.cloned.1.call-start
  74.3 0.1 copy.34
  74.5 12.3 %all-to-all-done.1 = bf16[8,48,512]{2,1,0:T(8,128)(2,1)S(1)} async-done(((bf16[8,48,512]{2,1,0:T(8,128)(2,1)}), bf16[8,48,512]{2,1,0:T(8,128)(2,1)S(1)}, u32[]{:S(2)}, u32[]{:S(2)}) %all-to-all-start.1) | async-done | bytes 393248 | tf_op jit(solution)/shard_map/all_to_all | solution.py:76
  86.8 0.5 mul.27
  87.2 0.9 fusion.2
  88.1 0.0 all-gather.2.cloned.1.call-update
  88.8 0.0 copy-done.4
  88.8 0.0 copy-done
  88.8 3.7 %gather_fusion = bf16[512,384]{1,0:T(8,128)(2,1)S(1)} fusion(bf16[4,128,384]{2,1,0:T(8,128)(2,1)S(1)} %bitcast.38, s32[512]{0:T(512)S(1)} %fusion.11), kind=kCustom, calls=%fused_computation | custom fusion | bytes 790528 | tf_op jit(solution)/shard_map/jit(take_along_axis)/gather | solution.py:20
  92.5 24.5 %all-gather.2.cloned.1.call-done = bf16[384,2048]{1,0:T(8,128)(2,1)} async-done(((bf16[384,512]{1,0:T(8,128)(2,1)}), bf16[384,2048]{1,0:T(8,128)(2,1)}) %all-gather.2.cloned.1.call-update) | async-done | bytes 1572880 | tf_op jit(solution)/shard_map/all_gather | solution.py:84
  117.1 4.0 %fusion = bf16[1,1,512,2048]{3,2,1,0:T(8,128)(2,1)} fusion(bf16[384,2048]{1,0:T(8,128)(2,1)} %all-gather.2.cloned.1.call-done, pred[512]{0:T(512)(128)(4,1)S(1)} %get-tuple-element.2, bf16[512,384]{1,0:T(8,128)(2,1)S(1)} %gather_fusion, pred[512]{0:T(512)(128)(4,1)S(1)} %get-tuple-element.3), kind=kOutput, calls=%fused_computation.2 | convolution fusion | flops 807600128 | bytes 4064256 | tf_op jit(solution)/shard_map/dot_general | solution.py:82
  (4 shorter events, 0.0 us)
Async XLA Ops:
  7.2 81.7 %copy-start = (bf16[1,1,512,384]{3,2,1,0:T(8,128)(2,1)S(1)}, bf16[1,1,512,384]{3,2,1,0:T(8,128)(2,1)}, u32[]{:S(2)}) copy-start(bf16[1,1,512,384]{3,2,1,0:T(8,128)(2,1)} %param.15) | copy-start | bytes 1179652
  7.2 42.2 %copy-start.1 = (f32[48,4,512]{2,1,0:T(4,128)S(1)}, f32[48,4,512]{2,1,0:T(4,128)}, u32[]{:S(2)}) copy-start(f32[48,4,512]{2,1,0:T(4,128)} %param.10) | copy-start | bytes 1179652
  7.2 37.5 %reduce-scatter.2.cloned.1.call-start = ((), (), s32[]{:S(2)}) async-start(), calls=%async_computation.4 | async-start | bytes 1966080 | tf_op jit(solution)/shard_map/reduce_scatter | solution.py:49
  7.2 43.1 %copy-start.6 = (s32[8,1]{0,1:T(1,128)S(1)}, s32[8,1]{0,1:T(1,128)}, u32[]{:S(2)}) copy-start(s32[8,1]{0,1:T(1,128)} %param.12) | copy-start | bytes 100
  44.7 20.6 %copy-start.2 = (f32[48,4,512]{2,1,0:T(4,128)S(1)}, f32[48,4,512]{2,1,0:T(4,128)}, u32[]{:S(2)}) copy-start(f32[48,4,512]{2,1,0:T(4,128)} %param.9) | copy-start | bytes 1179652
  44.7 20.6 %copy-start.5 = (s32[8,1]{0,1:T(1,128)S(1)}, s32[8,1]{0,1:T(1,128)}, u32[]{:S(2)}) copy-start(s32[8,1]{0,1:T(1,128)} %param.11) | copy-start | bytes 100
  44.7 17.3 %all-to-all-start = ((bf16[8,48,512]{2,1,0:T(8,128)(2,1)}), bf16[8,48,512]{2,1,0:T(8,128)(2,1)S(1)}, u32[]{:S(2)}, u32[]{:S(2)}) async-start(bf16[8,48,512]{2,1,0:T(8,128)(2,1)} %bitcast.42), calls=%async_computation.1 | async-start | bytes 786432 | tf_op jit(solution)/shard_map/all_to_all | solution.py:53
  62.0 8.9 %all-to-all-start.2 = ((bf16[8,48,4]{1,2,0:T(4,128)(2,1)}), bf16[8,48,4]{1,2,0:T(4,128)(2,1)S(1)}, u32[]{:S(2)}, u32[]{:S(2)}) async-start(bf16[8,48,4]{1,2,0:T(4,128)(2,1)} %copy.31), calls=%async_computation.3 | async-start | bytes 16384 | tf_op jit(solution)/shard_map/all_to_all | solution.py:77
  65.6 5.2 %copy-start.3 = (f32[48,4,512]{2,1,0:T(4,128)}, f32[48,4,512]{2,1,0:T(4,128)S(1)}, u32[]{:S(2)}) copy-start(f32[48,4,512]{2,1,0:T(4,128)S(1)} %fusion.1) | copy-start | bytes 1179652
  66.8 22.0 %copy-start.4 = (s32[1,1,4,128]{3,2,1,0:T(4,128)S(1)}, s32[1,1,4,128]{3,2,1,0:T(4,128)}, u32[]{:S(2)}) copy-start(s32[1,1,4,128]{3,2,1,0:T(4,128)} %param.14) | copy-start | bytes 6148
  70.8 15.9 %all-to-all-start.1 = ((bf16[8,48,512]{2,1,0:T(8,128)(2,1)}), bf16[8,48,512]{2,1,0:T(8,128)(2,1)S(1)}, u32[]{:S(2)}, u32[]{:S(2)}) async-start(bf16[8,48,512]{2,1,0:T(8,128)(2,1)} %copy.29), calls=%async_computation.2 | async-start | bytes 786432 | tf_op jit(solution)/shard_map/all_to_all | solution.py:76
  74.3 42.8 %all-gather.2.cloned.1.call-start = ((), (), s32[]{:S(2)}) async-start(), calls=%async_computation.5 | async-start | bytes 1966080 | tf_op jit(solution)/shard_map/all_gather | solution.py:84
Sparse Core Ops, SparseCore 0:
  11.0 33.6 reduce-scatter.1
  88.3 28.7 all-gather.1
where the time goes:
time: 128 us
  waiting for transfers between devices  88.5 us (69%)
  between operations  14.9 us (12%)
  starting transfers between devices  11.6 us (9%)
  local copies, waits for them, and re-layouts  6.73 us (5%)
  matrix products  4.88 us (4%)
  other arithmetic  1.4 us (1%)
    reduce_scatter x1, waiting for transfers between devices, shards(): lax.psum_scatter(gradient.astype(jnp.float32).astype(jnp.bfloat16), 'dp',...  36.7 us
    all_gather x1, waiting for transfers between devices, shards(): lax.all_gather(weight_cols, 'dp', axis=1, tiled=True)  24.5 us
    all_to_all x1, waiting for transfers between devices, shards(): lax.all_to_all(sent_values, 'expert', split_axis=0, concat_axis=0, tiled=...  12.3 us
    all_to_all x1, waiting for transfers between devices, shards(): lax.all_to_all(pieces.astype(jnp.bfloat16), 'expert', split_axis=0, conca...  10.3 us
    all_to_all x1, starting transfers between devices, shards(): lax.all_to_all(pieces.astype(jnp.bfloat16), 'expert', split_axis=0, conca...  4.72 us
    dot_general x1, matrix products, shards(): jnp.dot(selected, lax.all_gather(weight_cols, 'dp', axis=1, tiled=True),...  4.04 us
    all_to_all x1, waiting for transfers between devices, shards(): lax.all_to_all(sent_scales, 'expert', split_axis=0, concat_axis=0, tiled=...  3.97 us
    gather x1, local copies, waits for them, and re-layouts, select_rows(): picked = jnp.take_along_axis(blocked, route_index[0, 0][:, :, None], axis=1)  3.68 us
  transfers between devices with their start and end apart: 5, of which 5 were waited for; matrix products, arithmetic and copies ran while one was open for 6% of the time, Pallas kernels for 0%

commit v1 on v0

v1 whole, which is shorter than its diff:
```python
import functools

import jax
import jax.numpy as jnp
from jax import lax
from jax.experimental import pallas as pl
from jax.experimental.pallas import tpu as pltpu
from jax.sharding import PartitionSpec as P

QBLOCK = 128
momentum_decay = 0.9
step_rate = 0.5
epsilon = 1e-06
range_limit = 448.0
f32, bf16 = jnp.float32, jnp.bfloat16


def select_kernel(live_ref, index_ref, act_ref, out_ref):
    blocks, size = index_ref.shape
    for q in range(blocks):
        rows = lax.broadcasted_iota(jnp.int32, (size, size), 0)
        hot = (rows == index_ref[q : q + 1, :]).astype(f32).astype(bf16)
        picked = lax.dot_general(
            hot, act_ref[q * size : (q + 1) * size, :], (((0,), (0,)), ((), ())), preferred_element_type=f32
        )
        at = lax.broadcasted_iota(jnp.int32, picked.shape, 0) + q * size
        out_ref[q * size : (q + 1) * size, :] = jnp.where(at < live_ref[0, 0], picked, 0.0).astype(bf16)


def select_rows(activations, route_index, live_counts):
    rows, hidden = activations.shape
    return pl.pallas_call(
        select_kernel,
        out_shape=jax.ShapeDtypeStruct((rows, hidden), bf16),
        in_specs=[
            pl.BlockSpec(memory_space=pltpu.SMEM),
            pl.BlockSpec(memory_space=pltpu.VMEM),
            pl.BlockSpec(memory_space=pltpu.VMEM),
        ],
        out_specs=pl.BlockSpec(memory_space=pltpu.VMEM),
    )(live_counts, route_index, activations)


def product_kernel(count_j, count_k, place_ref, sel_ref, *refs):
    pieces = refs[: count_j * count_k]
    out_ref, weight, result, sems = refs[count_j * count_k :]
    e, d = place_ref[0], place_ref[1]
    half = pieces[0].shape[0] // 2
    columns = pieces[0].shape[1]
    copies = []
    for k in range(count_k):
        for j in range(count_j):
            for t in range(2):
                row = pl.multiple_of((e ^ (2 * j + t)) * half, 16)
                weight[k, pl.ds(row, half), :] = pieces[j * count_k + k][t * half : (t + 1) * half, :]
        result[k] = jnp.dot(sel_ref[...], weight[k], preferred_element_type=f32).astype(bf16)
        at = pl.multiple_of((d ^ k) * columns, 128)
        copy = pltpu.make_async_copy(result.at[k], out_ref.at[:, pl.ds(at, columns)], sems.at[k])
        copy.start()
        copies.append(copy)
    for copy in copies:
        copy.wait()


def multiply(place, selected, pieces):
    count_j, count_k = len(pieces), len(pieces[0])
    rows, hidden = selected.shape
    columns = pieces[0][0].shape[1]
    flat = [v for group in pieces for v in group]
    vmem = pl.BlockSpec(memory_space=pltpu.VMEM)
    return pl.pallas_call(
        functools.partial(product_kernel, count_j, count_k),
        out_shape=jax.ShapeDtypeStruct((rows, columns * count_k), bf16),
        in_specs=[pl.BlockSpec(memory_space=pltpu.SMEM), vmem] + [vmem] * len(flat),
        out_specs=pl.BlockSpec(memory_space=pl.ANY),
        scratch_shapes=[
            pltpu.VMEM((count_k, hidden, columns), bf16),
            pltpu.VMEM((count_k, rows, columns), bf16),
            pltpu.SemaphoreType.DMA((count_k,)),
        ],
        compiler_params=pltpu.CompilerParams(vmem_limit_bytes=24 * 1024 * 1024),
    )(place, selected, *flat)


def step_kernel(place_ref, current_ref, next_ref, momentum_ref, master_ref, theirs_ref, *refs):
    count = theirs_ref.shape[0]
    kept, (new_ref, mine_ref, other_ref, totals, restored) = refs[:count], refs[count:]
    e = place_ref[0]
    rows = theirs_ref.shape[1]
    experts, _, columns = totals.shape
    totals[...] = jnp.zeros_like(totals)
    for q in range(2 * count):
        j, t = q // 2, q % 2
        piece = theirs_ref[j] if t else kept[j][:rows, :]
        x = current_ref[e ^ q, 0]
        totals[x] += piece.astype(f32)
    for x in range(experts):
        new = momentum_decay * momentum_ref[x] + totals[x]
        new_ref[x] = new
        master = master_ref[x]
        weights = master - step_rate * new
        for b in range(columns // QBLOCK):
            part = slice(b * QBLOCK, (b + 1) * QBLOCK)
            top = jnp.max(jnp.abs(master[:, part]), axis=1, keepdims=True)
            scale = (top / range_limit + epsilon).astype(bf16).astype(f32)
            quant = jnp.clip(weights[:, part] / scale, -range_limit, range_limit).astype(bf16)
            restored[x, :, part] = (quant.astype(f32) * scale).astype(bf16)
    for q in range(2 * count):
        j, t = q // 2, q % 2
        out = other_ref if t else mine_ref
        out[j] = restored[next_ref[e ^ q, 0]]


def step(place, current_slots, next_slots, momentum, master, theirs, kept):
    smem = pl.BlockSpec(memory_space=pltpu.SMEM)
    vmem = pl.BlockSpec(memory_space=pltpu.VMEM)
    sent = jax.ShapeDtypeStruct(theirs.shape, bf16)
    return pl.pallas_call(
        step_kernel,
        out_shape=(jax.ShapeDtypeStruct(momentum.shape, f32), sent, sent),
        in_specs=[smem] * 3 + [vmem] * (3 + len(kept)),
        out_specs=(vmem,) * 3,
        scratch_shapes=[pltpu.VMEM(momentum.shape, f32), pltpu.VMEM(momentum.shape, bf16)],
        compiler_params=pltpu.CompilerParams(vmem_limit_bytes=16 * 1024 * 1024),
    )(place, current_slots, next_slots, momentum, master, theirs, *kept)


def plain_plan(slot_grads, momentum, master_weights, current_slots, next_slots):
    expert_count = lax.axis_size("expert")
    gradient = slot_grads[0, 0]
    hidden_rows = gradient.shape[0]
    slice_rows = hidden_rows // expert_count
    experts, columns = momentum.shape[1:]
    labels = jnp.arange(experts, dtype=jnp.int32)
    owner_table = current_slots[:, 0][None, :] == labels[:, None]
    summed = lax.psum_scatter(gradient, "dp", scatter_dimension=1, tiled=True)
    pieces = summed.reshape(expert_count, slice_rows, columns)
    received = lax.all_to_all(pieces, "expert", split_axis=0, concat_axis=0, tiled=True).astype(f32)
    totals = jnp.einsum("xs,spk->pxk", owner_table.astype(f32), received, precision=lax.Precision.HIGHEST)
    new_momentum = momentum_decay * momentum + totals
    weights = master_weights - step_rate * new_momentum
    blocks = weights.reshape(slice_rows, experts, columns // QBLOCK, QBLOCK)
    previous = master_weights.reshape(slice_rows, experts, columns // QBLOCK, QBLOCK)
    scales = (jnp.max(jnp.abs(previous), axis=3) / range_limit + epsilon).astype(bf16)
    scales = scales.astype(f32)[:, :, :, None]
    quantized = jnp.clip(blocks / scales, -range_limit, range_limit).astype(bf16)
    restored = (quantized.astype(f32) * scales).astype(bf16).reshape(slice_rows, experts, columns)
    chooser = (next_slots[:, 0][:, None] == labels[None, :]).astype(bf16)
    sent = jnp.einsum("sx,pxk->spk", chooser, restored, preferred_element_type=f32).astype(bf16)
    got = lax.all_to_all(sent, "expert", split_axis=0, concat_axis=0, tiled=True)
    weight = lax.all_gather(got.reshape(hidden_rows, columns), "dp", axis=1, tiled=True)
    return new_momentum, weight


def staged_shards(slot_grads, momentum, master_weights, current_slots, next_slots, live_counts, route_index, activations):
    ne = lax.axis_size("expert")
    nd = lax.axis_size("dp")
    e = lax.axis_index("expert")
    d = lax.axis_index("dp")
    grad = slot_grads[0, 0]
    hid = grad.shape[0]
    sr = hid // ne
    nx = momentum.shape[1]
    cols = momentum.shape[2]
    nj = ne // 2
    ob = lax.optimization_barrier
    place = jnp.stack([e, d])

    def after(value, *deps):
        return ob((value, *deps))[0]

    def dperm(v, k):
        return lax.ppermute(v, "dp", [(i, i ^ k) for i in range(nd)])

    def eperm(v, q):
        return lax.ppermute(v, "expert", [(i, i ^ q) for i in range(ne)])

    def blk(js, ks, g):
        return jnp.concatenate(
            [lax.dynamic_slice(g, ((e ^ (2 * j + t)) * sr, (d ^ k) * cols), (sr, cols)) for k in ks for j in js for t in (0, 1)], 0
        )

    def add(*vs):
        out = vs[0].astype(f32)
        for v in vs[1:]:
            out = out + v.astype(f32)
        return out.astype(bf16)

    recv = {}
    n2 = 2 * sr
    far = (3, 2)
    fx, fy, fd = (blk(far, (k,), grad) for k in (1, 2, 3))
    grad = after(grad, fx, fy, fd)
    own_far = blk(far, (0,), grad)
    s1 = blk((1,), (1, 3), grad)
    s0 = blk((0,), (2, 3), grad)
    o1x, o1 = blk((1,), (2,), grad), blk((1,), (0,), grad)
    o0x, o0 = blk((0,), (1,), grad), blk((0,), (0,), grad)
    rfx = dperm(fx, 1)
    rfy = dperm(fy, 2)
    rfd = dperm(fd, 3)
    r1 = dperm(after(s1, rfx), 1)
    r0 = dperm(after(s0, rfy), 2)
    tfar = add(own_far, rfx, rfy, rfd)
    z3 = eperm(tfar[:n2], 6)
    z2 = eperm(tfar[n2:], 4)
    q1 = dperm(after(add(o1x, r1[n2:]), tfar), 2)
    q0 = dperm(after(add(o0x, r0[n2:]), tfar), 1)
    t1 = add(o1, r1[:n2], q1)
    z1 = eperm(after(t1, z3), 2)
    t0 = add(o0, r0[:n2], q0)
    recv = {0: t0, 1: z1, 2: z2, 3: z3}
    mom_t, mas_t = momentum.transpose(1, 0, 2), master_weights.transpose(1, 0, 2)
    theirs = eperm(jnp.stack([recv[j][sr:] for j in range(nj)]), 1)
    new_mom, mine, other = step(place, current_slots, next_slots, mom_t, mas_t, theirs, [recv[j] for j in range(nj)])
    got = eperm(other, 1)
    w = [jnp.concatenate([mine[j], got[j]], 0) for j in range(nj)]
    v = [w[0]] + [eperm(w[j], 2 * j) for j in (1, 2, 3)]
    ox = dperm(v[0], 1)
    y1 = dperm(v[1], 2)
    oy = dperm(jnp.concatenate([after(v[0], ox), ox], 0), 2)
    x1 = dperm(jnp.concatenate([after(v[1], y1), y1], 0), 1)
    vf = jnp.concatenate([v[2], v[3]], 0)
    gx = dperm(after(vf, x1), 1)
    gy = dperm(after(vf, oy), 2)
    gd = dperm(after(vf, oy, x1), 3)
    full = [
        [v[0], ox, oy[:n2], oy[n2:]],
        [v[1], x1[:n2], y1, x1[n2:]],
        [v[2], gx[:n2], gy[:n2], gd[:n2]],
        [v[3], gx[n2:], gy[n2:], gd[n2:]],
    ]
    new_mom = after(new_mom, ox)
    sel = select_rows(activations[0, 0], route_index[0, 0], live_counts)
    out = multiply(place, sel, full)
    return new_mom.transpose(1, 0, 2), out[None, None]


def plain_shards(slot_grads, momentum, master_weights, current_slots, next_slots, live_counts, route_index, activations):
    new_momentum, weight = plain_plan(slot_grads, momentum, master_weights, current_slots, next_slots)
    selected = select_rows(activations[0, 0], route_index[0, 0], live_counts)
    product = jnp.dot(selected, weight, preferred_element_type=f32)
    return new_momentum, product.astype(bf16)[None, None]


def solution(mesh):
    in_specs = (
        P("dp", "expert", None, None), P("expert", None, "dp"), P("expert", None, "dp"), P(), P(), P("dp", "expert"),
        P("dp", "expert", None, None), P("dp", "expert", None, None),
    )
    out_specs = (P("expert", None, "dp"), P("dp", "expert", None, None))
    staged = mesh.shape["dp"] == 4 and mesh.shape["expert"] == 8
    shards = staged_shards if staged else plain_shards
    return jax.shard_map(shards, mesh=mesh, in_specs=in_specs, out_specs=out_specs, check_vma=False)
```

time: 128 us -> 74.6 us (0.58)
  waiting for transfers between devices: 88.5 us -> 36.5 us
  starting transfers between devices: 11.6 us -> 27.2 us
  between operations: 14.9 us -> 1.58 us
  Pallas kernels: 0 us -> 5.78 us
  matrix products: 4.88 us -> 0 us
  local copies, waits for them, and re-layouts: 6.73 us -> 2.92 us
    reduce_scatter x1 -> x0, waiting for transfers between devices: 36.7 us -> none  [shards(): lax.psum_scatter(gradient.astype(jnp.float32).astype(jnp.bfloat16), 'dp',...]
    ppermute x0 -> x22, waiting for transfers between devices: none -> 36.5 us  [the longest x14 27.2 us: dperm(): return lax.ppermute(v, 'dp', [(i, i ^ k) for i in range(nd)])]
    ppermute x0 -> x22, starting transfers between devices: none -> 27.2 us  [the longest x14 17.8 us: dperm(): return lax.ppermute(v, 'dp', [(i, i ^ k) for i in range(nd)])]
    all_to_all x3 -> x0, waiting for transfers between devices: 26.5 us -> none  [the longest x1 12.3 us: shards(): lax.all_to_all(sent_values, 'expert', split_axis=0, concat_axis=0, tiled=...]
    all_gather x1 -> x0, waiting for transfers between devices: 24.5 us -> none  [shards(): lax.all_gather(weight_cols, 'dp', axis=1, tiled=True)]
    all_to_all x3 -> x0, starting transfers between devices: 11.5 us -> none  [the longest x1 4.72 us: shards(): lax.all_to_all(pieces.astype(jnp.bfloat16), 'expert', split_axis=0, conca...]
    pallas_call x0 -> x3, Pallas kernels: none -> 5.78 us  [the longest x1 2.68 us: multiply(): pl.pallas_call(functools.partial(product_kernel, count_j, count_k), out_s...]
    dot_general x4 -> x0, matrix products: 4.88 us -> none  [the longest x1 4.04 us: shards(): jnp.dot(selected, lax.all_gather(weight_cols, 'dp', axis=1, tiled=True),...]
  transfers between devices with their start and end apart: 5 -> 22, of which waited for: 5 -> 15; matrix products, arithmetic and copies ran while one was open for 6% -> 3% of each run, Pallas kernels for 0% -> 3%
where the time goes in v1:
time: 74.6 us; the launch traced here: 74.4 us
  waiting for transfers between devices  36.5 us (49%)
  starting transfers between devices  27.2 us (36%)
  Pallas kernels  5.78 us (8%)
  local copies, waits for them, and re-layouts  2.92 us (4%)
  between operations  1.58 us (2%)
    ppermute x14, waiting for transfers between devices, dperm(): return lax.ppermute(v, 'dp', [(i, i ^ k) for i in range(nd)])  27.2 us
    ppermute x14, starting transfers between devices, dperm(): return lax.ppermute(v, 'dp', [(i, i ^ k) for i in range(nd)])  17.8 us
    ppermute x8, starting transfers between devices, eperm(): return lax.ppermute(v, 'expert', [(i, i ^ q) for i in range(ne)])  9.41 us
    ppermute x8, waiting for transfers between devices, eperm(): return lax.ppermute(v, 'expert', [(i, i ^ q) for i in range(ne)])  9.25 us
    pallas_call x1, Pallas kernels, multiply(): pl.pallas_call(functools.partial(product_kernel, count_j, count_k), out_s...  2.68 us
    pallas_call x1, Pallas kernels, select_rows(): pl.pallas_call(select_kernel, out_shape=jax.ShapeDtypeStruct((rows, hidde...  2.06 us
  transfers between devices with their start and end apart: 22, of which 15 were waited for; matrix products, arithmetic and copies ran while one was open for 3% of the time, Pallas kernels for 3%

profile of v1, /device:TPU:0, one launch (start us, length us, event | category | flops | bytes accessed | tf_op | source)
XLA Modules:
  0.0 74.4 jit_solution(2452744299118724500)
XLA Ops:
  0.7 1.2 %dynamic-slice_bitcast_fusion.11 = (bf16[48,512]{1,0:T(8,128)(2,1)S(1)}, bf16[48,512]{1,0:T(8,128)(2,1)S(1)}, bf16[48,512]{1,0:T(8,128)(2,1)S(1)}, bf16[48,512]{...) fusion(bf16[1,1,384,2048]{3,2,1,0:T(8,128)(2,1)} %param.8, ...), kind=kLoop, calls=%fused_computation.42 | loop fusion | bytes 1179676 | tf_op jit(solution)/shard_map/dynamic_slice | solution.py:180
  2.0 3.0 %collective-permute-start = (bf16[192,512]{1,0:T(8,128)(2,1)S(1)}, bf16[192,512]{1,0:T(8,128)(2,1)S(1)}, u32[]{:S(2)}, u32[]{:S(2)}) collective-permute-start(bf16[192,512]{1,0:T(8,128)(2,1)S(1)} %pad_maximum_fusion.1), channel_id=1, source_target_pairs={{0,16},{8,24},{16,0},{24,8},{1,17},{9,25},{17,1},{25,9},{2,18},{10... | collective-permute-start | bytes 589832 | tf_op jit(solution)/shard_map/ppermute | solution.py:173
  5.0 1.5 %collective-permute-start.3 = (bf16[192,512]{1,0:T(8,128)(2,1)S(1)}, bf16[192,512]{1,0:T(8,128)(2,1)S(1)}, u32[]{:S(2)}, u32[]{:S(2)}) collective-permute-start(bf16[192,512]{1,0:T(8,128)(2,1)S(1)} %pad_maximum_fusion.2), channel_id=1, source_target_pairs={{0,24},{8,16},{16,8},{24,0},{1,25},{9,17},{17,9},{25,1},{2,26},{10... | collective-permute-start | bytes 589832 | tf_op jit(solution)/shard_map/ppermute | solution.py:173
  6.5 0.1 collective-permute-start.2
  7.3 0.1 copy.12.current_ref
  7.4 0.1 copy.13.next_ref
  7.5 2.1 %shard_map.96.sel_ref = bf16[512,384]{1,0:T(8,128)(2,1)} custom-call(s32[1,1]{1,0:T(1,128)S(6)} %copy.18.live_ref, s32[4,128]{1,0:T(4,128)} %bitcast.63, bf16[512,384]{1,0:T(8,128)(2,1)} %bitcast.62), custom_call_target="tpu_custom_call" | custom-call | tf_op jit(solution)/shard_map/pallas_call | solution.py:32
  9.6 0.1 fusion
  9.7 4.4 %collective-permute-done = bf16[192,512]{1,0:T(8,128)(2,1)S(1)} collective-permute-done((bf16[192,512]{1,0:T(8,128)(2,1)S(1)}, bf16[192,512]{1,0:T(8,128)(2,1)S(1)}, u32[]{:S(2)}, u32[]{:S(2)}) %collective-permute-start) | collective-permute-done | bytes 196640 | tf_op jit(solution)/shard_map/ppermute | solution.py:173
  14.1 1.3 %collective-permute-done.2 = bf16[192,512]{1,0:T(8,128)(2,1)S(1)} collective-permute-done((bf16[192,512]{1,0:T(8,128)(2,1)S(1)}, bf16[192,512]{1,0:T(8,128)(2,1)S(1)}, u32[]{:S(2)}, u32[]{:S(2)}) %collective-permute-start.2) | collective-permute-done | bytes 196640 | tf_op jit(solution)/shard_map/ppermute | solution.py:173
  15.5 0.1 add_convert_fusion
  15.6 2.8 %collective-permute-start.9 = (bf16[96,512]{1,0:T(8,128)(2,1)S(1)}, bf16[96,512]{1,0:T(8,128)(2,1)S(1)}, u32[]{:S(2)}, u32[]{:S(2)}) collective-permute-start(bf16[96,512]{1,0:T(8,128)(2,1)S(1)} %get-tuple-element.84), channel_id=1, source_target_pairs={{0,4},{1,5},{2,6},{3,7},{4,0},{5,1},{6,2},{7,3},{8,12},{9,13},{10,... | collective-permute-start | bytes 294920 | tf_op jit(solution)/shard_map/ppermute | solution.py:176
  18.4 0.1 pad_add_fusion.place_ref
  18.5 1.3 %collective-permute-start.7 = (bf16[96,512]{1,0:T(8,128)(2,1)S(1)}, bf16[96,512]{1,0:T(8,128)(2,1)S(1)}, u32[]{:S(2)}, u32[]{:S(2)}) collective-permute-start(bf16[96,512]{1,0:T(8,128)(2,1)S(1)} %get-tuple-element.85), channel_id=1, source_target_pairs={{0,6},{1,7},{2,4},{3,5},{4,2},{5,3},{6,0},{7,1},{8,14},{9,15},{10,... | collective-permute-start | bytes 294920 | tf_op jit(solution)/shard_map/ppermute | solution.py:176
  19.9 1.5 %collective-permute-start.1 = (bf16[192,512]{1,0:T(8,128)(2,1)S(1)}, bf16[192,512]{1,0:T(8,128)(2,1)S(1)}, u32[]{:S(2)}, u32[]{:S(2)}) collective-permute-start(bf16[192,512]{1,0:T(8,128)(2,1)S(1)} %pad_maximum_fusion.3), channel_id=1, source_target_pairs={{0,16},{8,24},{16,0},{24,8},{1,17},{9,25},{17,1},{25,9},{2,18},{10... | collective-permute-start | bytes 589832 | tf_op jit(solution)/shard_map/ppermute | solution.py:173
  21.4 1.5 %collective-permute-start.5 = (bf16[192,512]{1,0:T(8,128)(2,1)S(1)}, bf16[192,512]{1,0:T(8,128)(2,1)S(1)}, u32[]{:S(2)}, u32[]{:S(2)}) collective-permute-start(bf16[192,512]{1,0:T(8,128)(2,1)S(1)} %pad_maximum_fusion.4), channel_id=1, source_target_pairs={{0,8},{8,0},{16,24},{24,16},{1,9},{9,1},{17,25},{25,17},{2,10},{10... | collective-permute-start | bytes 589832 | tf_op jit(solution)/shard_map/ppermute | solution.py:173
  22.9 2.4 %collective-permute-done.9.refs_2_ = bf16[96,512]{1,0:T(8,128)(2,1)S(1)} collective-permute-done((bf16[96,512]{1,0:T(8,128)(2,1)S(1)}, bf16[96,512]{1,0:T(8,128)(2,1)S(1)}, u32[]{:S(2)}, u32[]{:S(2)}) %collective-permute-start.9) | collective-permute-done | bytes 98336 | tf_op jit(solution)/shard_map/ppermute | solution.py:176
  25.3 1.8 %collective-permute-done.5 = bf16[192,512]{1,0:T(8,128)(2,1)S(1)} collective-permute-done((bf16[192,512]{1,0:T(8,128)(2,1)S(1)}, bf16[192,512]{1,0:T(8,128)(2,1)S(1)}, u32[]{:S(2)}, u32[]{:S(2)}) %collective-permute-start.5) | collective-permute-done | bytes 196640 | tf_op jit(solution)/shard_map/ppermute | solution.py:173
  27.1 0.6 collective-permute-start.6
  27.7 1.6 %collective-permute-start.4 = (bf16[96,512]{1,0:T(8,128)(2,1)S(1)}, bf16[96,512]{1,0:T(8,128)(2,1)S(1)}, u32[]{:S(2)}, u32[]{:S(2)}) collective-permute-start(bf16[96,512]{1,0:T(8,128)(2,1)S(1)} %add_convert_fusion.4), channel_id=1, source_target_pairs={{0,8},{8,0},{16,24},{24,16},{1,9},{9,1},{17,25},{25,17},{2,10},{10... | collective-permute-start | bytes 294920 | tf_op jit(solution)/shard_map/ppermute | solution.py:173
  29.2 2.5 %collective-permute-done.6 = bf16[96,512]{1,0:T(8,128)(2,1)S(1)} collective-permute-done((bf16[96,512]{1,0:T(8,128)(2,1)S(1)}, bf16[96,512]{1,0:T(8,128)(2,1)S(1)}, u32[]{:S(2)}, u32[]{:S(2)}) %collective-permute-start.6) | collective-permute-done | bytes 98336 | tf_op jit(solution)/shard_map/ppermute | solution.py:173
  31.8 0.4 collective-permute-start.8
  32.2 0.2 collective-permute-done.4
  32.4 4.1 %collective-permute-done.8.refs_1_ = bf16[96,512]{1,0:T(8,128)(2,1)S(1)} collective-permute-done((bf16[96,512]{1,0:T(8,128)(2,1)S(1)}, bf16[96,512]{1,0:T(8,128)(2,1)S(1)}, u32[]{:S(2)}, u32[]{:S(2)}) %collective-permute-start.8) | collective-permute-done | bytes 98336 | tf_op jit(solution)/shard_map/ppermute | solution.py:176
  36.5 0.1 collective-permute-start.10
  36.6 0.2 copy_bitcast_fusion
  36.9 1.2 %collective-permute-done.10.theirs_ref = bf16[4,48,512]{2,1,0:T(8,128)(2,1)S(1)} collective-permute-done((bf16[4,48,512]{2,1,0:T(8,128)(2,1)S(1)}, bf16[4,48,512]{2,1,0:T(8,128)(2,1)S(1)}, u32[]{:S(2)}, u32[]{:S(2)}) %collective-permute-start.10) | collective-permute-done | bytes 196640 | tf_op jit(solution)/shard_map/ppermute | solution.py:176
  38.0 1.0 %shard_map.95 = (f32[4,48,512]{2,1,0:T(8,128)S(1)}, bf16[4,48,512]{2,1,0:T(8,128)(2,1)S(1)}, bf16[4,48,512]{2,1,0:T(8,128)(2,1)S(1)}) custom-call(s32[2]{0:T(128)S(1)} %pad_add_fusion.place_ref, s32[8,1]{1,0:T(8,128)S(1)} %copy.12.current_ref, s32[8,1]{1,0:T(8,128)S(1)} %copy.13.next_ref, f32[4,48,512]{2,1,0:T(8,128)S(1)} %get-tuple-element.87.momentum_ref, ...), custom_call_target="tpu_custom_call" | custom-call | tf_op jit(solution)/shard_map/pallas_call | solution.py:118
  39.1 0.2 collective-permute-start.11
  39.3 1.3 %collective-permute-done.11 = bf16[4,48,512]{2,1,0:T(8,128)(2,1)S(1)} collective-permute-done((bf16[4,48,512]{2,1,0:T(8,128)(2,1)S(1)}, bf16[4,48,512]{2,1,0:T(8,128)(2,1)S(1)}, u32[]{:S(2)}, u32[]{:S(2)}) %collective-permute-start.11) | collective-permute-done | bytes 196640 | tf_op jit(solution)/shard_map/ppermute | solution.py:176
  40.6 0.4 collective-permute-start.14
  41.0 2.8 %collective-permute-start.17 = (bf16[96,512]{1,0:T(8,128)(2,1)S(1)}, bf16[96,512]{1,0:T(8,128)(2,1)S(1)}, u32[]{:S(2)}, u32[]{:S(2)}) collective-permute-start(bf16[96,512]{1,0:T(8,128)(2,1)S(1)} %pad_maximum_fusion.10), channel_id=1, source_target_pairs={{0,4},{1,5},{2,6},{3,7},{4,0},{5,1},{6,2},{7,3},{8,12},{9,13},{10,... | collective-permute-start | bytes 294920 | tf_op jit(solution)/shard_map/ppermute | solution.py:176
  43.8 1.6 %collective-permute-start.12 = (bf16[96,512]{1,0:T(8,128)(2,1)S(1)}, bf16[96,512]{1,0:T(8,128)(2,1)S(1)}, u32[]{:S(2)}, u32[]{:S(2)}) collective-permute-start(bf16[96,512]{1,0:T(8,128)(2,1)S(1)} %pad_maximum_fusion.8.refs_0_), channel_id=1, source_target_pairs={{0,8},{8,0},{16,24},{24,16},{1,9},{9,1},{17,25},{25,17},{2,10},{10... | collective-permute-start | bytes 294920 | tf_op jit(solution)/shard_map/ppermute | solution.py:173
  45.4 1.4 %collective-permute-start.18 = (bf16[96,512]{1,0:T(8,128)(2,1)S(1)}, bf16[96,512]{1,0:T(8,128)(2,1)S(1)}, u32[]{:S(2)}, u32[]{:S(2)}) collective-permute-start(bf16[96,512]{1,0:T(8,128)(2,1)S(1)} %pad_maximum_fusion.11), channel_id=1, source_target_pairs={{0,6},{1,7},{2,4},{3,5},{4,2},{5,3},{6,0},{7,1},{8,14},{9,15},{10,... | collective-permute-start | bytes 294920 | tf_op jit(solution)/shard_map/ppermute | solution.py:176
  46.8 1.7 %collective-permute-done.12.refs_1_ = bf16[96,512]{1,0:T(8,128)(2,1)S(1)} collective-permute-done((bf16[96,512]{1,0:T(8,128)(2,1)S(1)}, bf16[96,512]{1,0:T(8,128)(2,1)S(1)}, u32[]{:S(2)}, u32[]{:S(2)}) %collective-permute-start.12) | collective-permute-done | bytes 98336 | tf_op jit(solution)/shard_map/ppermute | solution.py:173
  48.5 1.0 %copy.14 = f32[48,4,512]{2,1,0:T(4,128)} copy(f32[48,4,512]{2,0,1:T(8,128)S(1)} %bitcast.59) | data formatting | bytes 786432
  49.5 0.6 collective-permute-start.13
  50.1 1.5 %collective-permute-start.15 = (bf16[96,512]{1,0:T(8,128)(2,1)S(1)}, bf16[96,512]{1,0:T(8,128)(2,1)S(1)}, u32[]{:S(2)}, u32[]{:S(2)}) collective-permute-start(bf16[96,512]{1,0:T(8,128)(2,1)S(1)} %collective-permute-done.14.refs_4_), channel_id=1, source_target_pairs={{0,16},{8,24},{16,0},{24,8},{1,17},{9,25},{17,1},{25,9},{2,18},{10... | collective-permute-start | bytes 294920 | tf_op jit(solution)/shard_map/ppermute | solution.py:173
  51.6 0.3 collective-permute-done.18.refs_12_
  52.0 5.2 %collective-permute-done.15.refs_6_ = bf16[96,512]{1,0:T(8,128)(2,1)S(1)} collective-permute-done((bf16[96,512]{1,0:T(8,128)(2,1)S(1)}, bf16[96,512]{1,0:T(8,128)(2,1)S(1)}, u32[]{:S(2)}, u32[]{:S(2)}) %collective-permute-start.15) | collective-permute-done | bytes 98336 | tf_op jit(solution)/shard_map/ppermute | solution.py:173
  57.2 1.6 %collective-permute-start.16 = (bf16[192,512]{1,0:T(8,128)(2,1)S(1)}, bf16[192,512]{1,0:T(8,128)(2,1)S(1)}, u32[]{:S(2)}, u32[]{:S(2)}) collective-permute-start(bf16[192,512]{1,0:T(8,128)(2,1)S(1)} %pad_maximum_fusion.7), channel_id=1, source_target_pairs={{0,8},{8,0},{16,24},{24,16},{1,9},{9,1},{17,25},{25,17},{2,10},{10... | collective-permute-start | bytes 589832 | tf_op jit(solution)/shard_map/ppermute | solution.py:173
  58.8 0.8 %collective-permute-start.20 = (bf16[192,512]{1,0:T(8,128)(2,1)S(1)}, bf16[192,512]{1,0:T(8,128)(2,1)S(1)}, u32[]{:S(2)}, u32[]{:S(2)}) collective-permute-start(bf16[192,512]{1,0:T(8,128)(2,1)S(1)} %constant_dynamic-update-slice_fusion), channel_id=1, source_target_pairs={{0,16},{8,24},{16,0},{24,8},{1,17},{9,25},{17,1},{25,9},{2,18},{10... | collective-permute-start | bytes 589832 | tf_op jit(solution)/shard_map/ppermute | solution.py:173
  59.6 4.0 %collective-permute-done.16 = bf16[192,512]{1,0:T(8,128)(2,1)S(1)} collective-permute-done((bf16[192,512]{1,0:T(8,128)(2,1)S(1)}, bf16[192,512]{1,0:T(8,128)(2,1)S(1)}, u32[]{:S(2)}, u32[]{:S(2)}) %collective-permute-start.16) | collective-permute-done | bytes 196640 | tf_op jit(solution)/shard_map/ppermute | solution.py:173
  63.7 1.5 %collective-permute-start.19 = (bf16[192,512]{1,0:T(8,128)(2,1)S(1)}, bf16[192,512]{1,0:T(8,128)(2,1)S(1)}, u32[]{:S(2)}, u32[]{:S(2)}) collective-permute-start(bf16[192,512]{1,0:T(8,128)(2,1)S(1)} %constant_dynamic-update-slice_fusion), channel_id=1, source_target_pairs={{0,8},{8,0},{16,24},{24,16},{1,9},{9,1},{17,25},{25,17},{2,10},{10... | collective-permute-start | bytes 589832 | tf_op jit(solution)/shard_map/ppermute | solution.py:173
  65.2 0.5 collective-permute-start.21
  65.7 3.6 %collective-permute-done.19 = bf16[192,512]{1,0:T(8,128)(2,1)S(1)} collective-permute-done((bf16[192,512]{1,0:T(8,128)(2,1)S(1)}, bf16[192,512]{1,0:T(8,128)(2,1)S(1)}, u32[]{:S(2)}, u32[]{:S(2)}) %collective-permute-start.19) | collective-permute-done | bytes 196640 | tf_op jit(solution)/shard_map/ppermute | solution.py:173
  69.3 2.4 %collective-permute-done.21 = bf16[192,512]{1,0:T(8,128)(2,1)S(1)} collective-permute-done((bf16[192,512]{1,0:T(8,128)(2,1)S(1)}, bf16[192,512]{1,0:T(8,128)(2,1)S(1)}, u32[]{:S(2)}, u32[]{:S(2)}) %collective-permute-start.21) | collective-permute-done | bytes 196640 | tf_op jit(solution)/shard_map/ppermute | solution.py:173
  71.8 2.7 %shard_map.97 = bf16[512,2048]{1,0:T(8,128)(2,1)} custom-call(s32[2]{0:T(128)S(1)} %pad_add_fusion.place_ref, bf16[512,384]{1,0:T(8,128)(2,1)S(1)} %copy-done, bf16[96,512]{1,0:T(8,128)(2,1)S(1)} %pad_maximum_fusion.8.refs_0_, bf16[96,512]{1,0:T(8,128)(2,1)S(1)} %collective-permute-done.12.refs_1_, bf16[96,512]{1,0:T(8,128)(2,1)S(1)} %get-tuple-element.83.refs_2_, ...), custom_call_target="tpu_custom_call" | custom-call | tf_op jit(solution)/shard_map/pallas_call | solution.py:71
  (49 shorter events, 0.5 us)
Async XLA Ops:
  0.6 6.7 %copy-start.4 = (s32[8,1]{0,1:T(1,128)S(1)}, s32[8,1]{0,1:T(1,128)}, u32[]{:S(2)}) copy-start(s32[8,1]{0,1:T(1,128)} %param.11) | copy-start | bytes 100
  0.6 6.8 %copy-start.5 = (s32[8,1]{0,1:T(1,128)S(1)}, s32[8,1]{0,1:T(1,128)}, u32[]{:S(2)}) copy-start(s32[8,1]{0,1:T(1,128)} %param.12) | copy-start | bytes 100
  0.7 8.9 %copy-start.1 = (bf16[1,1,384,2048]{3,2,1,0:T(8,128)(2,1)S(1)}, bf16[1,1,384,2048]{3,2,1,0:T(8,128)(2,1)}, u32[]{:S(2)}) copy-start(bf16[1,1,384,2048]{3,2,1,0:T(8,128)(2,1)} %param.8) | copy-start | bytes 4718596
  2.0 12.1 %collective-permute-start = (bf16[192,512]{1,0:T(8,128)(2,1)S(1)}, bf16[192,512]{1,0:T(8,128)(2,1)S(1)}, u32[]{:S(2)}, u32[]{:S(2)}) collective-permute-start(bf16[192,512]{1,0:T(8,128)(2,1)S(1)} %pad_maximum_fusion.1), channel_id=1, source_target_pairs={{0,16},{8,24},{16,0},{24,8},{1,17},{9,25},{17,1},{25,9},{2,18},{10... | collective-permute-start | bytes 589832 | tf_op jit(solution)/shard_map/ppermute | solution.py:173
  5.0 9.1 %collective-permute-start.3 = (bf16[192,512]{1,0:T(8,128)(2,1)S(1)}, bf16[192,512]{1,0:T(8,128)(2,1)S(1)}, u32[]{:S(2)}, u32[]{:S(2)}) collective-permute-start(bf16[192,512]{1,0:T(8,128)(2,1)S(1)} %pad_maximum_fusion.2), channel_id=1, source_target_pairs={{0,24},{8,16},{16,8},{24,0},{1,25},{9,17},{17,9},{25,1},{2,26},{10... | collective-permute-start | bytes 589832 | tf_op jit(solution)/shard_map/ppermute | solution.py:173
  6.5 8.9 %collective-permute-start.2 = (bf16[192,512]{1,0:T(8,128)(2,1)S(1)}, bf16[192,512]{1,0:T(8,128)(2,1)S(1)}, u32[]{:S(2)}, u32[]{:S(2)}) collective-permute-start(bf16[192,512]{1,0:T(8,128)(2,1)S(1)} %pad_maximum_fusion), channel_id=1, source_target_pairs={{0,8},{8,0},{16,24},{24,16},{1,9},{9,1},{17,25},{25,17},{2,10},{10... | collective-permute-start | bytes 589832 | tf_op jit(solution)/shard_map/ppermute | solution.py:173
  15.5 21.1 %copy-start.2 = (f32[48,4,512]{2,1,0:T(4,128)S(1)}, f32[48,4,512]{2,1,0:T(4,128)}, u32[]{:S(2)}) copy-start(f32[48,4,512]{2,1,0:T(4,128)} %param.10) | copy-start | bytes 1179652
  15.5 21.2 %copy-start.3 = (f32[48,4,512]{2,1,0:T(4,128)S(1)}, f32[48,4,512]{2,1,0:T(4,128)}, u32[]{:S(2)}) copy-start(f32[48,4,512]{2,1,0:T(4,128)} %param.9) | copy-start | bytes 1179652
  15.6 9.7 %collective-permute-start.9 = (bf16[96,512]{1,0:T(8,128)(2,1)S(1)}, bf16[96,512]{1,0:T(8,128)(2,1)S(1)}, u32[]{:S(2)}, u32[]{:S(2)}) collective-permute-start(bf16[96,512]{1,0:T(8,128)(2,1)S(1)} %get-tuple-element.84), channel_id=1, source_target_pairs={{0,4},{1,5},{2,6},{3,7},{4,0},{5,1},{6,2},{7,3},{8,12},{9,13},{10,... | collective-permute-start | bytes 294920 | tf_op jit(solution)/shard_map/ppermute | solution.py:176
  18.5 6.8 %collective-permute-start.7 = (bf16[96,512]{1,0:T(8,128)(2,1)S(1)}, bf16[96,512]{1,0:T(8,128)(2,1)S(1)}, u32[]{:S(2)}, u32[]{:S(2)}) collective-permute-start(bf16[96,512]{1,0:T(8,128)(2,1)S(1)} %get-tuple-element.85), channel_id=1, source_target_pairs={{0,6},{1,7},{2,4},{3,5},{4,2},{5,3},{6,0},{7,1},{8,14},{9,15},{10,... | collective-permute-start | bytes 294920 | tf_op jit(solution)/shard_map/ppermute | solution.py:176
  19.9 7.8 %collective-permute-start.1 = (bf16[192,512]{1,0:T(8,128)(2,1)S(1)}, bf16[192,512]{1,0:T(8,128)(2,1)S(1)}, u32[]{:S(2)}, u32[]{:S(2)}) collective-permute-start(bf16[192,512]{1,0:T(8,128)(2,1)S(1)} %pad_maximum_fusion.3), channel_id=1, source_target_pairs={{0,16},{8,24},{16,0},{24,8},{1,17},{9,25},{17,1},{25,9},{2,18},{10... | collective-permute-start | bytes 589832 | tf_op jit(solution)/shard_map/ppermute | solution.py:173
  21.4 5.7 %collective-permute-start.5 = (bf16[192,512]{1,0:T(8,128)(2,1)S(1)}, bf16[192,512]{1,0:T(8,128)(2,1)S(1)}, u32[]{:S(2)}, u32[]{:S(2)}) collective-permute-start(bf16[192,512]{1,0:T(8,128)(2,1)S(1)} %pad_maximum_fusion.4), channel_id=1, source_target_pairs={{0,8},{8,0},{16,24},{24,16},{1,9},{9,1},{17,25},{25,17},{2,10},{10... | collective-permute-start | bytes 589832 | tf_op jit(solution)/shard_map/ppermute | solution.py:173
  27.1 4.7 %collective-permute-start.6 = (bf16[96,512]{1,0:T(8,128)(2,1)S(1)}, bf16[96,512]{1,0:T(8,128)(2,1)S(1)}, u32[]{:S(2)}, u32[]{:S(2)}) collective-permute-start(bf16[96,512]{1,0:T(8,128)(2,1)S(1)} %add_convert_fusion.2), channel_id=1, source_target_pairs={{0,16},{8,24},{16,0},{24,8},{1,17},{9,25},{17,1},{25,9},{2,18},{10... | collective-permute-start | bytes 294920 | tf_op jit(solution)/shard_map/ppermute | solution.py:173
  27.7 4.7 %collective-permute-start.4 = (bf16[96,512]{1,0:T(8,128)(2,1)S(1)}, bf16[96,512]{1,0:T(8,128)(2,1)S(1)}, u32[]{:S(2)}, u32[]{:S(2)}) collective-permute-start(bf16[96,512]{1,0:T(8,128)(2,1)S(1)} %add_convert_fusion.4), channel_id=1, source_target_pairs={{0,8},{8,0},{16,24},{24,16},{1,9},{9,1},{17,25},{25,17},{2,10},{10... | collective-permute-start | bytes 294920 | tf_op jit(solution)/shard_map/ppermute | solution.py:173
  31.8 4.7 %collective-permute-start.8 = (bf16[96,512]{1,0:T(8,128)(2,1)S(1)}, bf16[96,512]{1,0:T(8,128)(2,1)S(1)}, u32[]{:S(2)}, u32[]{:S(2)}) collective-permute-start(bf16[96,512]{1,0:T(8,128)(2,1)S(1)} %add_convert_fusion.1), channel_id=1, source_target_pairs={{0,2},{1,3},{2,0},{3,1},{4,6},{5,7},{6,4},{7,5},{8,10},{9,11},{10,... | collective-permute-start | bytes 294920 | tf_op jit(solution)/shard_map/ppermute | solution.py:176
  36.5 1.5 %collective-permute-start.10 = (bf16[4,48,512]{2,1,0:T(8,128)(2,1)S(1)}, bf16[4,48,512]{2,1,0:T(8,128)(2,1)S(1)}, u32[]{:S(2)}, u32[]{:S(2)}) collective-permute-start(bf16[4,48,512]{2,1,0:T(8,128)(2,1)S(1)} %pad_maximum_fusion.5), channel_id=1, source_target_pairs={{0,1},{1,0},{2,3},{3,2},{4,5},{5,4},{6,7},{7,6},{8,9},{9,8},{10,11... | collective-permute-start | bytes 589832 | tf_op jit(solution)/shard_map/ppermute | solution.py:176
  39.1 1.5 %collective-permute-start.11 = (bf16[4,48,512]{2,1,0:T(8,128)(2,1)S(1)}, bf16[4,48,512]{2,1,0:T(8,128)(2,1)S(1)}, u32[]{:S(2)}, u32[]{:S(2)}) collective-permute-start(bf16[4,48,512]{2,1,0:T(8,128)(2,1)S(1)} %get-tuple-element.25), channel_id=1, source_target_pairs={{0,1},{1,0},{2,3},{3,2},{4,5},{5,4},{6,7},{7,6},{8,9},{9,8},{10,11... | collective-permute-start | bytes 589832 | tf_op jit(solution)/shard_map/ppermute | solution.py:176
  40.6 9.5 %collective-permute-start.14 = (bf16[96,512]{1,0:T(8,128)(2,1)S(1)}, bf16[96,512]{1,0:T(8,128)(2,1)S(1)}, u32[]{:S(2)}, u32[]{:S(2)}) collective-permute-start(bf16[96,512]{1,0:T(8,128)(2,1)S(1)} %pad_maximum_fusion.9), channel_id=1, source_target_pairs={{0,2},{1,3},{2,0},{3,1},{4,6},{5,7},{6,4},{7,5},{8,10},{9,11},{10,... | collective-permute-start | bytes 294920 | tf_op jit(solution)/shard_map/ppermute | solution.py:176
  41.0 10.6 %collective-permute-start.17 = (bf16[96,512]{1,0:T(8,128)(2,1)S(1)}, bf16[96,512]{1,0:T(8,128)(2,1)S(1)}, u32[]{:S(2)}, u32[]{:S(2)}) collective-permute-start(bf16[96,512]{1,0:T(8,128)(2,1)S(1)} %pad_maximum_fusion.10), channel_id=1, source_target_pairs={{0,4},{1,5},{2,6},{3,7},{4,0},{5,1},{6,2},{7,3},{8,12},{9,13},{10,... | collective-permute-start | bytes 294920 | tf_op jit(solution)/shard_map/ppermute | solution.py:176
  43.8 4.7 %collective-permute-start.12 = (bf16[96,512]{1,0:T(8,128)(2,1)S(1)}, bf16[96,512]{1,0:T(8,128)(2,1)S(1)}, u32[]{:S(2)}, u32[]{:S(2)}) collective-permute-start(bf16[96,512]{1,0:T(8,128)(2,1)S(1)} %pad_maximum_fusion.8.refs_0_), channel_id=1, source_target_pairs={{0,8},{8,0},{16,24},{24,16},{1,9},{9,1},{17,25},{25,17},{2,10},{10... | collective-permute-start | bytes 294920 | tf_op jit(solution)/shard_map/ppermute | solution.py:173
  45.4 6.6 %collective-permute-start.18 = (bf16[96,512]{1,0:T(8,128)(2,1)S(1)}, bf16[96,512]{1,0:T(8,128)(2,1)S(1)}, u32[]{:S(2)}, u32[]{:S(2)}) collective-permute-start(bf16[96,512]{1,0:T(8,128)(2,1)S(1)} %pad_maximum_fusion.11), channel_id=1, source_target_pairs={{0,6},{1,7},{2,4},{3,5},{4,2},{5,3},{6,0},{7,1},{8,14},{9,15},{10,... | collective-permute-start | bytes 294920 | tf_op jit(solution)/shard_map/ppermute | solution.py:176
  49.5 22.3 %copy-start = (bf16[512,384]{1,0:T(8,128)(2,1)S(1)}, bf16[512,384]{1,0:T(8,128)(2,1)}, u32[]{:S(2)}) copy-start(bf16[512,384]{1,0:T(8,128)(2,1)} %shard_map.96.sel_ref) | copy-start | bytes 1179652
  49.5 9.3 %collective-permute-start.13 = (bf16[192,512]{1,0:T(8,128)(2,1)S(1)}, bf16[192,512]{1,0:T(8,128)(2,1)S(1)}, u32[]{:S(2)}, u32[]{:S(2)}) collective-permute-start(bf16[192,512]{1,0:T(8,128)(2,1)S(1)} %pad_maximum_fusion.6), channel_id=1, source_target_pairs={{0,16},{8,24},{16,0},{24,8},{1,17},{9,25},{17,1},{25,9},{2,18},{10... | collective-permute-start | bytes 589832 | tf_op jit(solution)/shard_map/ppermute | solution.py:173
  50.1 7.1 %collective-permute-start.15 = (bf16[96,512]{1,0:T(8,128)(2,1)S(1)}, bf16[96,512]{1,0:T(8,128)(2,1)S(1)}, u32[]{:S(2)}, u32[]{:S(2)}) collective-permute-start(bf16[96,512]{1,0:T(8,128)(2,1)S(1)} %collective-permute-done.14.refs_4_), channel_id=1, source_target_pairs={{0,16},{8,24},{16,0},{24,8},{1,17},{9,25},{17,1},{25,9},{2,18},{10... | collective-permute-start | bytes 294920 | tf_op jit(solution)/shard_map/ppermute | solution.py:173
  57.2 6.4 %collective-permute-start.16 = (bf16[192,512]{1,0:T(8,128)(2,1)S(1)}, bf16[192,512]{1,0:T(8,128)(2,1)S(1)}, u32[]{:S(2)}, u32[]{:S(2)}) collective-permute-start(bf16[192,512]{1,0:T(8,128)(2,1)S(1)} %pad_maximum_fusion.7), channel_id=1, source_target_pairs={{0,8},{8,0},{16,24},{24,16},{1,9},{9,1},{17,25},{25,17},{2,10},{10... | collective-permute-start | bytes 589832 | tf_op jit(solution)/shard_map/ppermute | solution.py:173
  58.8 6.9 %collective-permute-start.20 = (bf16[192,512]{1,0:T(8,128)(2,1)S(1)}, bf16[192,512]{1,0:T(8,128)(2,1)S(1)}, u32[]{:S(2)}, u32[]{:S(2)}) collective-permute-start(bf16[192,512]{1,0:T(8,128)(2,1)S(1)} %constant_dynamic-update-slice_fusion), channel_id=1, source_target_pairs={{0,16},{8,24},{16,0},{24,8},{1,17},{9,25},{17,1},{25,9},{2,18},{10... | collective-permute-start | bytes 589832 | tf_op jit(solution)/shard_map/ppermute | solution.py:173
  63.7 5.7 %collective-permute-start.19 = (bf16[192,512]{1,0:T(8,128)(2,1)S(1)}, bf16[192,512]{1,0:T(8,128)(2,1)S(1)}, u32[]{:S(2)}, u32[]{:S(2)}) collective-permute-start(bf16[192,512]{1,0:T(8,128)(2,1)S(1)} %constant_dynamic-update-slice_fusion), channel_id=1, source_target_pairs={{0,8},{8,0},{16,24},{24,16},{1,9},{9,1},{17,25},{25,17},{2,10},{10... | collective-permute-start | bytes 589832 | tf_op jit(solution)/shard_map/ppermute | solution.py:173
  65.2 6.6 %collective-permute-start.21 = (bf16[192,512]{1,0:T(8,128)(2,1)S(1)}, bf16[192,512]{1,0:T(8,128)(2,1)S(1)}, u32[]{:S(2)}, u32[]{:S(2)}) collective-permute-start(bf16[192,512]{1,0:T(8,128)(2,1)S(1)} %constant_dynamic-update-slice_fusion), channel_id=1, source_target_pairs={{0,24},{8,16},{16,8},{24,0},{1,25},{9,17},{17,9},{25,1},{2,26},{10... | collective-permute-start | bytes 589832 | tf_op jit(solution)/shard_map/ppermute | solution.py:173

commit v2 on v1

--- a/solution.py
+++ b/solution.py
@@ -163,6 +163,7 @@
     nx = momentum.shape[1]
     cols = momentum.shape[2]
     nj = ne // 2
+    n2 = 2 * sr
     ob = lax.optimization_barrier
     place = jnp.stack([e, d])
 
@@ -186,51 +187,55 @@
             out = out + v.astype(f32)
         return out.astype(bf16)
 
-    recv = {}
-    n2 = 2 * sr
-    far = (3, 2)
-    fx, fy, fd = (blk(far, (k,), grad) for k in (1, 2, 3))
-    grad = after(grad, fx, fy, fd)
-    own_far = blk(far, (0,), grad)
-    s1 = blk((1,), (1, 3), grad)
-    s0 = blk((0,), (2, 3), grad)
-    o1x, o1 = blk((1,), (2,), grad), blk((1,), (0,), grad)
-    o0x, o0 = blk((0,), (1,), grad), blk((0,), (0,), grad)
-    rfx = dperm(fx, 1)
-    rfy = dperm(fy, 2)
-    rfd = dperm(fd, 3)
-    r1 = dperm(after(s1, rfx), 1)
-    r0 = dperm(after(s0, rfy), 2)
-    tfar = add(own_far, rfx, rfy, rfd)
-    z3 = eperm(tfar[:n2], 6)
-    z2 = eperm(tfar[n2:], 4)
-    q1 = dperm(after(add(o1x, r1[n2:]), tfar), 2)
-    q0 = dperm(after(add(o0x, r0[n2:]), tfar), 1)
-    t1 = add(o1, r1[:n2], q1)
-    z1 = eperm(after(t1, z3), 2)
-    t0 = add(o0, r0[:n2], q0)
+    sx3 = blk((3,), (1, 3), grad)
+    sy2 = blk((2,), (2, 3), grad)
+    grad = after(grad, sx3, sy2)
+    ox3, o3 = blk((3,), (2,), grad), blk((3,), (0,), grad)
+    oy2, o2 = blk((2,), (1,), grad), blk((2,), (0,), grad)
+    sx1 = blk((1,), (1, 3), grad)
+    sy0 = blk((0,), (2, 3), grad)
+    ox1, o1 = blk((1,), (2,), grad), blk((1,), (0,), grad)
+    oy0, o0 = blk((0,), (1,), grad), blk((0,), (0,), grad)
+    x3 = dperm(sx3, 1)
+    y2 = dperm(sy2, 2)
+    x1 = dperm(sx1, 1)
+    y0 = dperm(sy0, 2)
+    y3 = dperm(add(ox3, x3[n2:]), 2)
+    x2 = dperm(add(oy2, y2[n2:]), 1)
+    t3 = add(o3, x3[:n2], y3)
+    t2 = add(o2, y2[:n2], x2)
+    z3 = eperm(t3, 6)
+    z2 = eperm(t2, 4)
+    y1 = dperm(add(ox1, x1[n2:]), 2)
+    x0 = dperm(add(oy0, y0[n2:]), 1)
+    t1 = add(o1, x1[:n2], y1)
+    z1 = eperm(t1, 2)
+    t0 = add(after(o0, z3, z2), y0[:n2], x0)
     recv = {0: t0, 1: z1, 2: z2, 3: z3}
     mom_t, mas_t = momentum.transpose(1, 0, 2), master_weights.transpose(1, 0, 2)
     theirs = eperm(jnp.stack([recv[j][sr:] for j in range(nj)]), 1)
     new_mom, mine, other = step(place, current_slots, next_slots, mom_t, mas_t, theirs, [recv[j] for j in range(nj)])
     got = eperm(other, 1)
     w = [jnp.concatenate([mine[j], got[j]], 0) for j in range(nj)]
-    v = [w[0]] + [eperm(w[j], 2 * j) for j in (1, 2, 3)]
-    ox = dperm(v[0], 1)
-    y1 = dperm(v[1], 2)
-    oy = dperm(jnp.concatenate([after(v[0], ox), ox], 0), 2)
-    x1 = dperm(jnp.concatenate([after(v[1], y1), y1], 0), 1)
-    vf = jnp.concatenate([v[2], v[3]], 0)
-    gx = dperm(after(vf, x1), 1)
-    gy = dperm(after(vf, oy), 2)
-    gd = dperm(after(vf, oy, x1), 3)
-    full = [
-        [v[0], ox, oy[:n2], oy[n2:]],
-        [v[1], x1[:n2], y1, x1[n2:]],
-        [v[2], gx[:n2], gy[:n2], gd[:n2]],
-        [v[3], gx[n2:], gy[n2:], gd[n2:]],
-    ]
-    new_mom = after(new_mom, ox)
+    v = [w[0], None, None, None]
+    v[1] = eperm(w[1], 2)
+    v[2] = eperm(w[2], 4)
+    v[3] = eperm(w[3], 6)
+    full = [None] * 4
+    ax0 = dperm(v[0], 1)
+    by0 = dperm(v[1], 2)
+    ay0 = dperm(jnp.concatenate([v[0], ax0], 0), 2)
+    bx0 = dperm(jnp.concatenate([v[1], by0], 0), 1)
+    full[0] = [v[0], ax0, ay0[:n2], ay0[n2:]]
+    full[1] = [v[1], bx0[:n2], by0, bx0[n2:]]
+    ax1 = dperm(v[2], 1)
+    by1 = dperm(v[3], 2)
+    ay1 = dperm(jnp.concatenate([v[2], ax1], 0), 2)
+    bx1 = dperm(jnp.concatenate([v[3], by1], 0), 1)
+    full[2] = [v[2], ax1, ay1[:n2], ay1[n2:]]
+    full[3] = [v[3], bx1[:n2], by1, bx1[n2:]]
+    late = ay0
+    new_mom = after(new_mom, late)
     sel = select_rows(activations[0, 0], route_index[0, 0], live_counts)
     out = multiply(place, sel, full)
     return new_mom.transpose(1, 0, 2), out[None, None]

time: 74.6 us -> 60.1 us (0.81)
  waiting for transfers between devices: 36.5 us -> 19.4 us
  starting transfers between devices: 27.2 us -> 29.8 us
    ppermute x14 -> x16, waiting for transfers between devices: 27.2 us -> 7.3 us  [dperm(): return lax.ppermute(v, 'dp', [(i, i ^ k) for i in range(nd)])]
    ppermute x8, waiting for transfers between devices: 9.25 us -> 12.1 us  [eperm(): return lax.ppermute(v, 'expert', [(i, i ^ q) for i in range(ne)])]
    ppermute x14 -> x16, starting transfers between devices: 17.8 us -> 20.4 us  [dperm(): return lax.ppermute(v, 'dp', [(i, i ^ k) for i in range(nd)])]
  transfers between devices with their start and end apart: 22 -> 24, of which waited for: 15 -> 13; matrix products, arithmetic and copies ran while one was open for 3% -> 3% of each run, Pallas kernels for 3% -> 3%
where the time goes in v2:
time: 60.1 us; the launch traced here: 59.9 us
  starting transfers between devices  29.8 us (50%)
  waiting for transfers between devices  19.4 us (32%)
  Pallas kernels  5.78 us (10%)
  local copies, waits for them, and re-layouts  2.8 us (5%)
  between operations  1.6 us (3%)
    ppermute x16, starting transfers between devices, dperm(): return lax.ppermute(v, 'dp', [(i, i ^ k) for i in range(nd)])  20.4 us
    ppermute x8, waiting for transfers between devices, eperm(): return lax.ppermute(v, 'expert', [(i, i ^ q) for i in range(ne)])  12.1 us
    ppermute x8, starting transfers between devices, eperm(): return lax.ppermute(v, 'expert', [(i, i ^ q) for i in range(ne)])  9.47 us
    ppermute x16, waiting for transfers between devices, dperm(): return lax.ppermute(v, 'dp', [(i, i ^ k) for i in range(nd)])  7.3 us
    pallas_call x1, Pallas kernels, multiply(): pl.pallas_call(functools.partial(product_kernel, count_j, count_k), out_s...  2.68 us
    pallas_call x1, Pallas kernels, select_rows(): pl.pallas_call(select_kernel, out_shape=jax.ShapeDtypeStruct((rows, hidde...  2.06 us
    dynamic_slice x2, local copies, waits for them, and re-layouts, blk(): lax.dynamic_slice(g, ((e ^ 2 * j + t) * sr, (d ^ k) * cols), (sr, cols))  1.27 us
  transfers between devices with their start and end apart: 24, of which 13 were waited for; matrix products, arithmetic and copies ran while one was open for 3% of the time, Pallas kernels for 3%

profile of v2, /device:TPU:0, one launch (start us, length us, event | category | flops | bytes accessed | tf_op | source)
XLA Modules:
  0.0 59.9 jit_solution(611912226204098916)
XLA Ops:
  0.7 1.1 %dynamic-slice_bitcast_fusion.3 = (bf16[48,512]{1,0:T(8,128)(2,1)S(1)}, bf16[48,512]{1,0:T(8,128)(2,1)S(1)}, bf16[48,512]{1,0:T(8,128)(2,1)S(1)}, bf16[48,512]{1...) fusion(bf16[1,1,384,2048]{3,2,1,0:T(8,128)(2,1)} %param.8, ...), kind=kLoop, calls=%fused_computation.39 | loop fusion | bytes 786460 | tf_op jit(solution)/shard_map/dynamic_slice | solution.py:181
  1.8 3.0 %collective-permute-start = (bf16[192,512]{1,0:T(8,128)(2,1)S(1)}, bf16[192,512]{1,0:T(8,128)(2,1)S(1)}, u32[]{:S(2)}, u32[]{:S(2)}) collective-permute-start(bf16[192,512]{1,0:T(8,128)(2,1)S(1)} %pad_maximum_fusion), channel_id=1, source_target_pairs={{0,8},{8,0},{16,24},{24,16},{1,9},{9,1},{17,25},{25,17},{2,10},{10... | collective-permute-start | bytes 589832 | tf_op jit(solution)/shard_map/ppermute | solution.py:174
  4.9 1.6 %collective-permute-start.3 = (bf16[192,512]{1,0:T(8,128)(2,1)S(1)}, bf16[192,512]{1,0:T(8,128)(2,1)S(1)}, u32[]{:S(2)}, u32[]{:S(2)}) collective-permute-start(bf16[192,512]{1,0:T(8,128)(2,1)S(1)} %pad_maximum_fusion.1), channel_id=1, source_target_pairs={{0,16},{8,24},{16,0},{24,8},{1,17},{9,25},{17,1},{25,9},{2,18},{10... | collective-permute-start | bytes 589832 | tf_op jit(solution)/shard_map/ppermute | solution.py:174
  6.4 0.2 fusion
  6.6 0.6 collective-permute-start.6
  7.2 0.2 collective-permute-start.8
  8.1 0.1 copy.12.current_ref
  8.2 0.1 copy.13.next_ref
  8.3 2.1 %shard_map.96.sel_ref = bf16[512,384]{1,0:T(8,128)(2,1)} custom-call(s32[1,1]{1,0:T(1,128)S(6)} %copy.17.live_ref, s32[4,128]{1,0:T(4,128)} %bitcast.55, bf16[512,384]{1,0:T(8,128)(2,1)} %bitcast.54), custom_call_target="tpu_custom_call" | custom-call | tf_op jit(solution)/shard_map/pallas_call | solution.py:32
  10.3 0.1 pad_add_fusion.place_ref
  10.4 0.1 collective-permute-done
  10.6 2.1 %collective-permute-start.1 = (bf16[96,512]{1,0:T(8,128)(2,1)S(1)}, bf16[96,512]{1,0:T(8,128)(2,1)S(1)}, u32[]{:S(2)}, u32[]{:S(2)}) collective-permute-start(bf16[96,512]{1,0:T(8,128)(2,1)S(1)} %add_convert_fusion.7), channel_id=1, source_target_pairs={{0,16},{8,24},{16,0},{24,8},{1,17},{9,25},{17,1},{25,9},{2,18},{10... | collective-permute-start | bytes 294920 | tf_op jit(solution)/shard_map/ppermute | solution.py:174
  12.6 0.1 collective-permute-done.3
  12.8 1.6 %collective-permute-start.4 = (bf16[96,512]{1,0:T(8,128)(2,1)S(1)}, bf16[96,512]{1,0:T(8,128)(2,1)S(1)}, u32[]{:S(2)}, u32[]{:S(2)}) collective-permute-start(bf16[96,512]{1,0:T(8,128)(2,1)S(1)} %add_convert_fusion.5), channel_id=1, source_target_pairs={{0,8},{8,0},{16,24},{24,16},{1,9},{9,1},{17,25},{25,17},{2,10},{10... | collective-permute-start | bytes 294920 | tf_op jit(solution)/shard_map/ppermute | solution.py:174
  14.3 2.2 %collective-permute-done.6 = bf16[192,512]{1,0:T(8,128)(2,1)S(1)} collective-permute-done((bf16[192,512]{1,0:T(8,128)(2,1)S(1)}, bf16[192,512]{1,0:T(8,128)(2,1)S(1)}, u32[]{:S(2)}, u32[]{:S(2)}) %collective-permute-start.6) | collective-permute-done | bytes 196640 | tf_op jit(solution)/shard_map/ppermute | solution.py:174
  16.6 0.4 collective-permute-start.7
  17.0 1.8 %collective-permute-start.9 = (bf16[96,512]{1,0:T(8,128)(2,1)S(1)}, bf16[96,512]{1,0:T(8,128)(2,1)S(1)}, u32[]{:S(2)}, u32[]{:S(2)}) collective-permute-start(bf16[96,512]{1,0:T(8,128)(2,1)S(1)} %add_convert_fusion.1), channel_id=1, source_target_pairs={{0,16},{8,24},{16,0},{24,8},{1,17},{9,25},{17,1},{25,9},{2,18},{10... | collective-permute-start | bytes 294920 | tf_op jit(solution)/shard_map/ppermute | solution.py:174
  18.8 3.7 %collective-permute-start.2 = (bf16[96,512]{1,0:T(8,128)(2,1)S(1)}, bf16[96,512]{1,0:T(8,128)(2,1)S(1)}, u32[]{:S(2)}, u32[]{:S(2)}) collective-permute-start(bf16[96,512]{1,0:T(8,128)(2,1)S(1)} %add_convert_fusion.6), channel_id=1, source_target_pairs={{0,6},{1,7},{2,4},{3,5},{4,2},{5,3},{6,0},{7,1},{8,14},{9,15},{10,... | collective-permute-start | bytes 294920 | tf_op jit(solution)/shard_map/ppermute | solution.py:177
  22.6 0.1 collective-permute-start.5
  22.7 0.9 %collective-permute-start.10 = (bf16[96,512]{1,0:T(8,128)(2,1)S(1)}, bf16[96,512]{1,0:T(8,128)(2,1)S(1)}, u32[]{:S(2)}, u32[]{:S(2)}) collective-permute-start(bf16[96,512]{1,0:T(8,128)(2,1)S(1)} %add_convert_fusion), channel_id=1, source_target_pairs={{0,2},{1,3},{2,0},{3,1},{4,6},{5,7},{6,4},{7,5},{8,10},{9,11},{10,... | collective-permute-start | bytes 294920 | tf_op jit(solution)/shard_map/ppermute | solution.py:177
  23.6 2.5 %collective-permute-done.2.refs_3_ = bf16[96,512]{1,0:T(8,128)(2,1)S(1)} collective-permute-done((bf16[96,512]{1,0:T(8,128)(2,1)S(1)}, bf16[96,512]{1,0:T(8,128)(2,1)S(1)}, u32[]{:S(2)}, u32[]{:S(2)}) %collective-permute-start.2) | collective-permute-done | bytes 98336 | tf_op jit(solution)/shard_map/ppermute | solution.py:177
  26.1 2.5 %collective-permute-done.5.refs_2_ = bf16[96,512]{1,0:T(8,128)(2,1)S(1)} collective-permute-done((bf16[96,512]{1,0:T(8,128)(2,1)S(1)}, bf16[96,512]{1,0:T(8,128)(2,1)S(1)}, u32[]{:S(2)}, u32[]{:S(2)}) %collective-permute-start.5) | collective-permute-done | bytes 98336 | tf_op jit(solution)/shard_map/ppermute | solution.py:177
  28.7 0.1 collective-permute-start.11
  28.8 0.2 copy_bitcast_fusion
  29.1 1.2 %collective-permute-done.11.theirs_ref = bf16[4,48,512]{2,1,0:T(8,128)(2,1)S(1)} collective-permute-done((bf16[4,48,512]{2,1,0:T(8,128)(2,1)S(1)}, bf16[4,48,512]{2,1,0:T(8,128)(2,1)S(1)}, u32[]{:S(2)}, u32[]{:S(2)}) %collective-permute-start.11) | collective-permute-done | bytes 196640 | tf_op jit(solution)/shard_map/ppermute | solution.py:177
  30.2 1.0 %shard_map.95 = (f32[4,48,512]{2,1,0:T(8,128)S(1)}, bf16[4,48,512]{2,1,0:T(8,128)(2,1)S(1)}, bf16[4,48,512]{2,1,0:T(8,128)(2,1)S(1)}) custom-call(s32[2]{0:T(128)S(1)} %pad_add_fusion.place_ref, s32[8,1]{1,0:T(8,128)S(1)} %copy.12.current_ref, s32[8,1]{1,0:T(8,128)S(1)} %copy.13.next_ref, f32[4,48,512]{2,1,0:T(8,128)S(1)} %get-tuple-element.65.momentum_ref, ...), custom_call_target="tpu_custom_call" | custom-call | tf_op jit(solution)/shard_map/pallas_call | solution.py:118
  31.3 0.2 collective-permute-start.12
  31.5 1.3 %collective-permute-done.12 = bf16[4,48,512]{2,1,0:T(8,128)(2,1)S(1)} collective-permute-done((bf16[4,48,512]{2,1,0:T(8,128)(2,1)S(1)}, bf16[4,48,512]{2,1,0:T(8,128)(2,1)S(1)}, u32[]{:S(2)}, u32[]{:S(2)}) %collective-permute-start.12) | collective-permute-done | bytes 196640 | tf_op jit(solution)/shard_map/ppermute | solution.py:177
  32.8 1.4 %collective-permute-start.13 = (bf16[96,512]{1,0:T(8,128)(2,1)S(1)}, bf16[96,512]{1,0:T(8,128)(2,1)S(1)}, u32[]{:S(2)}, u32[]{:S(2)}) collective-permute-start(bf16[96,512]{1,0:T(8,128)(2,1)S(1)} %pad_maximum_fusion.10.refs_0_), channel_id=1, source_target_pairs={{0,8},{8,0},{16,24},{24,16},{1,9},{9,1},{17,25},{25,17},{2,10},{10... | collective-permute-start | bytes 294920 | tf_op jit(solution)/shard_map/ppermute | solution.py:174
  34.2 0.8 %collective-permute-start.15 = (bf16[96,512]{1,0:T(8,128)(2,1)S(1)}, bf16[96,512]{1,0:T(8,128)(2,1)S(1)}, u32[]{:S(2)}, u32[]{:S(2)}) collective-permute-start(bf16[96,512]{1,0:T(8,128)(2,1)S(1)} %pad_maximum_fusion.11), channel_id=1, source_target_pairs={{0,2},{1,3},{2,0},{3,1},{4,6},{5,7},{6,4},{7,5},{8,10},{9,11},{10,... | collective-permute-start | bytes 294920 | tf_op jit(solution)/shard_map/ppermute | solution.py:177
  35.0 2.1 %collective-permute-start.18 = (bf16[96,512]{1,0:T(8,128)(2,1)S(1)}, bf16[96,512]{1,0:T(8,128)(2,1)S(1)}, u32[]{:S(2)}, u32[]{:S(2)}) collective-permute-start(bf16[96,512]{1,0:T(8,128)(2,1)S(1)} %pad_maximum_fusion.12), channel_id=1, source_target_pairs={{0,4},{1,5},{2,6},{3,7},{4,0},{5,1},{6,2},{7,3},{8,12},{9,13},{10,... | collective-permute-start | bytes 294920 | tf_op jit(solution)/shard_map/ppermute | solution.py:177
  37.2 1.7 %collective-permute-start.21 = (bf16[96,512]{1,0:T(8,128)(2,1)S(1)}, bf16[96,512]{1,0:T(8,128)(2,1)S(1)}, u32[]{:S(2)}, u32[]{:S(2)}) collective-permute-start(bf16[96,512]{1,0:T(8,128)(2,1)S(1)} %pad_maximum_fusion.13), channel_id=1, source_target_pairs={{0,6},{1,7},{2,4},{3,5},{4,2},{5,3},{6,0},{7,1},{8,14},{9,15},{10,... | collective-permute-start | bytes 294920 | tf_op jit(solution)/shard_map/ppermute | solution.py:177
  38.8 1.2 %collective-permute-done.15.refs_4_ = bf16[96,512]{1,0:T(8,128)(2,1)S(1)} collective-permute-done((bf16[96,512]{1,0:T(8,128)(2,1)S(1)}, bf16[96,512]{1,0:T(8,128)(2,1)S(1)}, u32[]{:S(2)}, u32[]{:S(2)}) %collective-permute-start.15) | collective-permute-done | bytes 98336 | tf_op jit(solution)/shard_map/ppermute | solution.py:177
  40.1 0.8 %collective-permute-start.16 = (bf16[96,512]{1,0:T(8,128)(2,1)S(1)}, bf16[96,512]{1,0:T(8,128)(2,1)S(1)}, u32[]{:S(2)}, u32[]{:S(2)}) collective-permute-start(bf16[96,512]{1,0:T(8,128)(2,1)S(1)} %collective-permute-done.15.refs_4_), channel_id=1, source_target_pairs={{0,16},{8,24},{16,0},{24,8},{1,17},{9,25},{17,1},{25,9},{2,18},{10... | collective-permute-start | bytes 294920 | tf_op jit(solution)/shard_map/ppermute | solution.py:174
  40.9 1.3 %collective-permute-start.14 = (bf16[192,512]{1,0:T(8,128)(2,1)S(1)}, bf16[192,512]{1,0:T(8,128)(2,1)S(1)}, u32[]{:S(2)}, u32[]{:S(2)}) collective-permute-start(bf16[192,512]{1,0:T(8,128)(2,1)S(1)} %pad_maximum_fusion.5), channel_id=1, source_target_pairs={{0,16},{8,24},{16,0},{24,8},{1,17},{9,25},{17,1},{25,9},{2,18},{10... | collective-permute-start | bytes 589832 | tf_op jit(solution)/shard_map/ppermute | solution.py:174
  42.2 3.4 %collective-permute-done.18.refs_8_ = bf16[96,512]{1,0:T(8,128)(2,1)S(1)} collective-permute-done((bf16[96,512]{1,0:T(8,128)(2,1)S(1)}, bf16[96,512]{1,0:T(8,128)(2,1)S(1)}, u32[]{:S(2)}, u32[]{:S(2)}) %collective-permute-start.18) | collective-permute-done | bytes 98336 | tf_op jit(solution)/shard_map/ppermute | solution.py:177
  45.6 0.6 collective-permute-start.19
  46.1 1.4 %collective-permute-start.22 = (bf16[96,512]{1,0:T(8,128)(2,1)S(1)}, bf16[96,512]{1,0:T(8,128)(2,1)S(1)}, u32[]{:S(2)}, u32[]{:S(2)}) collective-permute-start(bf16[96,512]{1,0:T(8,128)(2,1)S(1)} %collective-permute-done.21.refs_12_), channel_id=1, source_target_pairs={{0,16},{8,24},{16,0},{24,8},{1,17},{9,25},{17,1},{25,9},{2,18},{10... | collective-permute-start | bytes 294920 | tf_op jit(solution)/shard_map/ppermute | solution.py:174
  47.5 0.0 copy-start
  47.6 1.3 %collective-permute-start.17 = (bf16[192,512]{1,0:T(8,128)(2,1)S(1)}, bf16[192,512]{1,0:T(8,128)(2,1)S(1)}, u32[]{:S(2)}, u32[]{:S(2)}) collective-permute-start(bf16[192,512]{1,0:T(8,128)(2,1)S(1)} %pad_maximum_fusion.6), channel_id=1, source_target_pairs={{0,8},{8,0},{16,24},{24,16},{1,9},{9,1},{17,25},{25,17},{2,10},{10... | collective-permute-start | bytes 589832 | tf_op jit(solution)/shard_map/ppermute | solution.py:174
  48.9 1.3 %collective-permute-done.19.refs_9_ = bf16[96,512]{1,0:T(8,128)(2,1)S(1)} collective-permute-done((bf16[96,512]{1,0:T(8,128)(2,1)S(1)}, bf16[96,512]{1,0:T(8,128)(2,1)S(1)}, u32[]{:S(2)}, u32[]{:S(2)}) %collective-permute-start.19) | collective-permute-done | bytes 98336 | tf_op jit(solution)/shard_map/ppermute | solution.py:174
  50.2 1.3 %collective-permute-start.20 = (bf16[192,512]{1,0:T(8,128)(2,1)S(1)}, bf16[192,512]{1,0:T(8,128)(2,1)S(1)}, u32[]{:S(2)}, u32[]{:S(2)}) collective-permute-start(bf16[192,512]{1,0:T(8,128)(2,1)S(1)} %pad_maximum_fusion.7), channel_id=1, source_target_pairs={{0,16},{8,24},{16,0},{24,8},{1,17},{9,25},{17,1},{25,9},{2,18},{10... | collective-permute-start | bytes 589832 | tf_op jit(solution)/shard_map/ppermute | solution.py:174
  51.5 1.1 %collective-permute-start.23 = (bf16[192,512]{1,0:T(8,128)(2,1)S(1)}, bf16[192,512]{1,0:T(8,128)(2,1)S(1)}, u32[]{:S(2)}, u32[]{:S(2)}) collective-permute-start(bf16[192,512]{1,0:T(8,128)(2,1)S(1)} %pad_maximum_fusion.8), channel_id=1, source_target_pairs={{0,8},{8,0},{16,24},{24,16},{1,9},{9,1},{17,25},{25,17},{2,10},{10... | collective-permute-start | bytes 589832 | tf_op jit(solution)/shard_map/ppermute | solution.py:174
  52.6 1.0 %copy.14 = f32[48,4,512]{2,1,0:T(4,128)} copy(f32[48,4,512]{2,0,1:T(8,128)S(1)} %bitcast.51) | data formatting | bytes 786432
  53.6 1.1 %collective-permute-done.17 = bf16[192,512]{1,0:T(8,128)(2,1)S(1)} collective-permute-done((bf16[192,512]{1,0:T(8,128)(2,1)S(1)}, bf16[192,512]{1,0:T(8,128)(2,1)S(1)}, u32[]{:S(2)}, u32[]{:S(2)}) %collective-permute-start.17) | collective-permute-done | bytes 196640 | tf_op jit(solution)/shard_map/ppermute | solution.py:174
  54.7 1.2 %collective-permute-done.20 = bf16[192,512]{1,0:T(8,128)(2,1)S(1)} collective-permute-done((bf16[192,512]{1,0:T(8,128)(2,1)S(1)}, bf16[192,512]{1,0:T(8,128)(2,1)S(1)}, u32[]{:S(2)}, u32[]{:S(2)}) %collective-permute-start.20) | collective-permute-done | bytes 196640 | tf_op jit(solution)/shard_map/ppermute | solution.py:174
  55.9 1.3 %collective-permute-done.23 = bf16[192,512]{1,0:T(8,128)(2,1)S(1)} collective-permute-done((bf16[192,512]{1,0:T(8,128)(2,1)S(1)}, bf16[192,512]{1,0:T(8,128)(2,1)S(1)}, u32[]{:S(2)}, u32[]{:S(2)}) %collective-permute-start.23) | collective-permute-done | bytes 196640 | tf_op jit(solution)/shard_map/ppermute | solution.py:174
  57.2 2.7 %shard_map.97 = bf16[512,2048]{1,0:T(8,128)(2,1)} custom-call(s32[2]{0:T(128)S(1)} %pad_add_fusion.place_ref, bf16[512,384]{1,0:T(8,128)(2,1)S(1)} %copy-done, bf16[96,512]{1,0:T(8,128)(2,1)S(1)} %pad_maximum_fusion.10.refs_0_, bf16[96,512]{1,0:T(8,128)(2,1)S(1)} %collective-permute-done.13.refs_1_, bf16[96,512]{1,0:T(8,128)(2,1)S(1)} %get-tuple-element.63.refs_2_, ...), custom_call_target="tpu_custom_call" | custom-call | tf_op jit(solution)/shard_map/pallas_call | solution.py:71
  (54 shorter events, 0.6 us)
Async XLA Ops:
  0.6 5.8 %copy-start.1 = (bf16[1,1,384,2048]{3,2,1,0:T(8,128)(2,1)S(1)}, bf16[1,1,384,2048]{3,2,1,0:T(8,128)(2,1)}, u32[]{:S(2)}) copy-start(bf16[1,1,384,2048]{3,2,1,0:T(8,128)(2,1)} %param.8) | copy-start | bytes 4718596
  1.8 8.7 %collective-permute-start = (bf16[192,512]{1,0:T(8,128)(2,1)S(1)}, bf16[192,512]{1,0:T(8,128)(2,1)S(1)}, u32[]{:S(2)}, u32[]{:S(2)}) collective-permute-start(bf16[192,512]{1,0:T(8,128)(2,1)S(1)} %pad_maximum_fusion), channel_id=1, source_target_pairs={{0,8},{8,0},{16,24},{24,16},{1,9},{9,1},{17,25},{25,17},{2,10},{10... | collective-permute-start | bytes 589832 | tf_op jit(solution)/shard_map/ppermute | solution.py:174
  4.9 7.9 %collective-permute-start.3 = (bf16[192,512]{1,0:T(8,128)(2,1)S(1)}, bf16[192,512]{1,0:T(8,128)(2,1)S(1)}, u32[]{:S(2)}, u32[]{:S(2)}) collective-permute-start(bf16[192,512]{1,0:T(8,128)(2,1)S(1)} %pad_maximum_fusion.1), channel_id=1, source_target_pairs={{0,16},{8,24},{16,0},{24,8},{1,17},{9,25},{17,1},{25,9},{2,18},{10... | collective-permute-start | bytes 589832 | tf_op jit(solution)/shard_map/ppermute | solution.py:174
  6.4 1.7 %copy-start.4 = (s32[8,1]{0,1:T(1,128)S(1)}, s32[8,1]{0,1:T(1,128)}, u32[]{:S(2)}) copy-start(s32[8,1]{0,1:T(1,128)} %param.11) | copy-start | bytes 100
  6.4 1.8 %copy-start.5 = (s32[8,1]{0,1:T(1,128)S(1)}, s32[8,1]{0,1:T(1,128)}, u32[]{:S(2)}) copy-start(s32[8,1]{0,1:T(1,128)} %param.12) | copy-start | bytes 100
  6.6 9.9 %collective-permute-start.6 = (bf16[192,512]{1,0:T(8,128)(2,1)S(1)}, bf16[192,512]{1,0:T(8,128)(2,1)S(1)}, u32[]{:S(2)}, u32[]{:S(2)}) collective-permute-start(bf16[192,512]{1,0:T(8,128)(2,1)S(1)} %pad_maximum_fusion.2), channel_id=1, source_target_pairs={{0,16},{8,24},{16,0},{24,8},{1,17},{9,25},{17,1},{25,9},{2,18},{10... | collective-permute-start | bytes 589832 | tf_op jit(solution)/shard_map/ppermute | solution.py:174
  7.2 9.7 %collective-permute-start.8 = (bf16[192,512]{1,0:T(8,128)(2,1)S(1)}, bf16[192,512]{1,0:T(8,128)(2,1)S(1)}, u32[]{:S(2)}, u32[]{:S(2)}) collective-permute-start(bf16[192,512]{1,0:T(8,128)(2,1)S(1)} %pad_maximum_fusion.3), channel_id=1, source_target_pairs={{0,8},{8,0},{16,24},{24,16},{1,9},{9,1},{17,25},{25,17},{2,10},{10... | collective-permute-start | bytes 589832 | tf_op jit(solution)/shard_map/ppermute | solution.py:174
  10.6 8.2 %collective-permute-start.1 = (bf16[96,512]{1,0:T(8,128)(2,1)S(1)}, bf16[96,512]{1,0:T(8,128)(2,1)S(1)}, u32[]{:S(2)}, u32[]{:S(2)}) collective-permute-start(bf16[96,512]{1,0:T(8,128)(2,1)S(1)} %add_convert_fusion.7), channel_id=1, source_target_pairs={{0,16},{8,24},{16,0},{24,8},{1,17},{9,25},{17,1},{25,9},{2,18},{10... | collective-permute-start | bytes 294920 | tf_op jit(solution)/shard_map/ppermute | solution.py:174
  12.7 16.1 %copy-start.2 = (f32[48,4,512]{2,1,0:T(4,128)S(1)}, f32[48,4,512]{2,1,0:T(4,128)}, u32[]{:S(2)}) copy-start(f32[48,4,512]{2,1,0:T(4,128)} %param.10) | copy-start | bytes 1179652
  12.7 16.1 %copy-start.3 = (f32[48,4,512]{2,1,0:T(4,128)S(1)}, f32[48,4,512]{2,1,0:T(4,128)}, u32[]{:S(2)}) copy-start(f32[48,4,512]{2,1,0:T(4,128)} %param.9) | copy-start | bytes 1179652
  12.8 9.7 %collective-permute-start.4 = (bf16[96,512]{1,0:T(8,128)(2,1)S(1)}, bf16[96,512]{1,0:T(8,128)(2,1)S(1)}, u32[]{:S(2)}, u32[]{:S(2)}) collective-permute-start(bf16[96,512]{1,0:T(8,128)(2,1)S(1)} %add_convert_fusion.5), channel_id=1, source_target_pairs={{0,8},{8,0},{16,24},{24,16},{1,9},{9,1},{17,25},{25,17},{2,10},{10... | collective-permute-start | bytes 294920 | tf_op jit(solution)/shard_map/ppermute | solution.py:174
  16.6 12.0 %collective-permute-start.7 = (bf16[96,512]{1,0:T(8,128)(2,1)S(1)}, bf16[96,512]{1,0:T(8,128)(2,1)S(1)}, u32[]{:S(2)}, u32[]{:S(2)}) collective-permute-start(bf16[96,512]{1,0:T(8,128)(2,1)S(1)} %add_convert_fusion.3), channel_id=1, source_target_pairs={{0,8},{8,0},{16,24},{24,16},{1,9},{9,1},{17,25},{25,17},{2,10},{10... | collective-permute-start | bytes 294920 | tf_op jit(solution)/shard_map/ppermute | solution.py:174
  17.0 5.6 %collective-permute-start.9 = (bf16[96,512]{1,0:T(8,128)(2,1)S(1)}, bf16[96,512]{1,0:T(8,128)(2,1)S(1)}, u32[]{:S(2)}, u32[]{:S(2)}) collective-permute-start(bf16[96,512]{1,0:T(8,128)(2,1)S(1)} %add_convert_fusion.1), channel_id=1, source_target_pairs={{0,16},{8,24},{16,0},{24,8},{1,17},{9,25},{17,1},{25,9},{2,18},{10... | collective-permute-start | bytes 294920 | tf_op jit(solution)/shard_map/ppermute | solution.py:174
  18.8 7.2 %collective-permute-start.2 = (bf16[96,512]{1,0:T(8,128)(2,1)S(1)}, bf16[96,512]{1,0:T(8,128)(2,1)S(1)}, u32[]{:S(2)}, u32[]{:S(2)}) collective-permute-start(bf16[96,512]{1,0:T(8,128)(2,1)S(1)} %add_convert_fusion.6), channel_id=1, source_target_pairs={{0,6},{1,7},{2,4},{3,5},{4,2},{5,3},{6,0},{7,1},{8,14},{9,15},{10,... | collective-permute-start | bytes 294920 | tf_op jit(solution)/shard_map/ppermute | solution.py:177
  22.6 6.0 %collective-permute-start.5 = (bf16[96,512]{1,0:T(8,128)(2,1)S(1)}, bf16[96,512]{1,0:T(8,128)(2,1)S(1)}, u32[]{:S(2)}, u32[]{:S(2)}) collective-permute-start(bf16[96,512]{1,0:T(8,128)(2,1)S(1)} %add_convert_fusion.4), channel_id=1, source_target_pairs={{0,4},{1,5},{2,6},{3,7},{4,0},{5,1},{6,2},{7,3},{8,12},{9,13},{10,... | collective-permute-start | bytes 294920 | tf_op jit(solution)/shard_map/ppermute | solution.py:177
  22.7 6.0 %collective-permute-start.10 = (bf16[96,512]{1,0:T(8,128)(2,1)S(1)}, bf16[96,512]{1,0:T(8,128)(2,1)S(1)}, u32[]{:S(2)}, u32[]{:S(2)}) collective-permute-start(bf16[96,512]{1,0:T(8,128)(2,1)S(1)} %add_convert_fusion), channel_id=1, source_target_pairs={{0,2},{1,3},{2,0},{3,1},{4,6},{5,7},{6,4},{7,5},{8,10},{9,11},{10,... | collective-permute-start | bytes 294920 | tf_op jit(solution)/shard_map/ppermute | solution.py:177
  28.7 1.5 %collective-permute-start.11 = (bf16[4,48,512]{2,1,0:T(8,128)(2,1)S(1)}, bf16[4,48,512]{2,1,0:T(8,128)(2,1)S(1)}, u32[]{:S(2)}, u32[]{:S(2)}) collective-permute-start(bf16[4,48,512]{2,1,0:T(8,128)(2,1)S(1)} %pad_maximum_fusion.4), channel_id=1, source_target_pairs={{0,1},{1,0},{2,3},{3,2},{4,5},{5,4},{6,7},{7,6},{8,9},{9,8},{10,11... | collective-permute-start | bytes 589832 | tf_op jit(solution)/shard_map/ppermute | solution.py:177
  31.3 1.5 %collective-permute-start.12 = (bf16[4,48,512]{2,1,0:T(8,128)(2,1)S(1)}, bf16[4,48,512]{2,1,0:T(8,128)(2,1)S(1)}, u32[]{:S(2)}, u32[]{:S(2)}) collective-permute-start(bf16[4,48,512]{2,1,0:T(8,128)(2,1)S(1)} %get-tuple-element.12), channel_id=1, source_target_pairs={{0,1},{1,0},{2,3},{3,2},{4,5},{5,4},{6,7},{7,6},{8,9},{9,8},{10,11... | collective-permute-start | bytes 589832 | tf_op jit(solution)/shard_map/ppermute | solution.py:177
  32.8 8.0 %collective-permute-start.13 = (bf16[96,512]{1,0:T(8,128)(2,1)S(1)}, bf16[96,512]{1,0:T(8,128)(2,1)S(1)}, u32[]{:S(2)}, u32[]{:S(2)}) collective-permute-start(bf16[96,512]{1,0:T(8,128)(2,1)S(1)} %pad_maximum_fusion.10.refs_0_), channel_id=1, source_target_pairs={{0,8},{8,0},{16,24},{24,16},{1,9},{9,1},{17,25},{25,17},{2,10},{10... | collective-permute-start | bytes 294920 | tf_op jit(solution)/shard_map/ppermute | solution.py:174
  34.2 5.8 %collective-permute-start.15 = (bf16[96,512]{1,0:T(8,128)(2,1)S(1)}, bf16[96,512]{1,0:T(8,128)(2,1)S(1)}, u32[]{:S(2)}, u32[]{:S(2)}) collective-permute-start(bf16[96,512]{1,0:T(8,128)(2,1)S(1)} %pad_maximum_fusion.11), channel_id=1, source_target_pairs={{0,2},{1,3},{2,0},{3,1},{4,6},{5,7},{6,4},{7,5},{8,10},{9,11},{10,... | collective-permute-start | bytes 294920 | tf_op jit(solution)/shard_map/ppermute | solution.py:177
  35.0 10.5 %collective-permute-start.18 = (bf16[96,512]{1,0:T(8,128)(2,1)S(1)}, bf16[96,512]{1,0:T(8,128)(2,1)S(1)}, u32[]{:S(2)}, u32[]{:S(2)}) collective-permute-start(bf16[96,512]{1,0:T(8,128)(2,1)S(1)} %pad_maximum_fusion.12), channel_id=1, source_target_pairs={{0,4},{1,5},{2,6},{3,7},{4,0},{5,1},{6,2},{7,3},{8,12},{9,13},{10,... | collective-permute-start | bytes 294920 | tf_op jit(solution)/shard_map/ppermute | solution.py:177
  37.2 9.0 %collective-permute-start.21 = (bf16[96,512]{1,0:T(8,128)(2,1)S(1)}, bf16[96,512]{1,0:T(8,128)(2,1)S(1)}, u32[]{:S(2)}, u32[]{:S(2)}) collective-permute-start(bf16[96,512]{1,0:T(8,128)(2,1)S(1)} %pad_maximum_fusion.13), channel_id=1, source_target_pairs={{0,6},{1,7},{2,4},{3,5},{4,2},{5,3},{6,0},{7,1},{8,14},{9,15},{10,... | collective-permute-start | bytes 294920 | tf_op jit(solution)/shard_map/ppermute | solution.py:177
  40.1 7.5 %collective-permute-start.16 = (bf16[96,512]{1,0:T(8,128)(2,1)S(1)}, bf16[96,512]{1,0:T(8,128)(2,1)S(1)}, u32[]{:S(2)}, u32[]{:S(2)}) collective-permute-start(bf16[96,512]{1,0:T(8,128)(2,1)S(1)} %collective-permute-done.15.refs_4_), channel_id=1, source_target_pairs={{0,16},{8,24},{16,0},{24,8},{1,17},{9,25},{17,1},{25,9},{2,18},{10... | collective-permute-start | bytes 294920 | tf_op jit(solution)/shard_map/ppermute | solution.py:174
  40.9 11.7 %collective-permute-start.14 = (bf16[192,512]{1,0:T(8,128)(2,1)S(1)}, bf16[192,512]{1,0:T(8,128)(2,1)S(1)}, u32[]{:S(2)}, u32[]{:S(2)}) collective-permute-start(bf16[192,512]{1,0:T(8,128)(2,1)S(1)} %pad_maximum_fusion.5), channel_id=1, source_target_pairs={{0,16},{8,24},{16,0},{24,8},{1,17},{9,25},{17,1},{25,9},{2,18},{10... | collective-permute-start | bytes 589832 | tf_op jit(solution)/shard_map/ppermute | solution.py:174
  45.6 4.6 %collective-permute-start.19 = (bf16[96,512]{1,0:T(8,128)(2,1)S(1)}, bf16[96,512]{1,0:T(8,128)(2,1)S(1)}, u32[]{:S(2)}, u32[]{:S(2)}) collective-permute-start(bf16[96,512]{1,0:T(8,128)(2,1)S(1)} %collective-permute-done.18.refs_8_), channel_id=1, source_target_pairs={{0,8},{8,0},{16,24},{24,16},{1,9},{9,1},{17,25},{25,17},{2,10},{10... | collective-permute-start | bytes 294920 | tf_op jit(solution)/shard_map/ppermute | solution.py:174
  46.1 5.3 %collective-permute-start.22 = (bf16[96,512]{1,0:T(8,128)(2,1)S(1)}, bf16[96,512]{1,0:T(8,128)(2,1)S(1)}, u32[]{:S(2)}, u32[]{:S(2)}) collective-permute-start(bf16[96,512]{1,0:T(8,128)(2,1)S(1)} %collective-permute-done.21.refs_12_), channel_id=1, source_target_pairs={{0,16},{8,24},{16,0},{24,8},{1,17},{9,25},{17,1},{25,9},{2,18},{10... | collective-permute-start | bytes 294920 | tf_op jit(solution)/shard_map/ppermute | solution.py:174
  47.5 9.7 %copy-start = (bf16[512,384]{1,0:T(8,128)(2,1)S(1)}, bf16[512,384]{1,0:T(8,128)(2,1)}, u32[]{:S(2)}) copy-start(bf16[512,384]{1,0:T(8,128)(2,1)} %shard_map.96.sel_ref) | copy-start | bytes 1179652
  47.6 7.2 %collective-permute-start.17 = (bf16[192,512]{1,0:T(8,128)(2,1)S(1)}, bf16[192,512]{1,0:T(8,128)(2,1)S(1)}, u32[]{:S(2)}, u32[]{:S(2)}) collective-permute-start(bf16[192,512]{1,0:T(8,128)(2,1)S(1)} %pad_maximum_fusion.6), channel_id=1, source_target_pairs={{0,8},{8,0},{16,24},{24,16},{1,9},{9,1},{17,25},{25,17},{2,10},{10... | collective-permute-start | bytes 589832 | tf_op jit(solution)/shard_map/ppermute | solution.py:174
  50.2 5.7 %collective-permute-start.20 = (bf16[192,512]{1,0:T(8,128)(2,1)S(1)}, bf16[192,512]{1,0:T(8,128)(2,1)S(1)}, u32[]{:S(2)}, u32[]{:S(2)}) collective-permute-start(bf16[192,512]{1,0:T(8,128)(2,1)S(1)} %pad_maximum_fusion.7), channel_id=1, source_target_pairs={{0,16},{8,24},{16,0},{24,8},{1,17},{9,25},{17,1},{25,9},{2,18},{10... | collective-permute-start | bytes 589832 | tf_op jit(solution)/shard_map/ppermute | solution.py:174
  51.5 5.7 %collective-permute-start.23 = (bf16[192,512]{1,0:T(8,128)(2,1)S(1)}, bf16[192,512]{1,0:T(8,128)(2,1)S(1)}, u32[]{:S(2)}, u32[]{:S(2)}) collective-permute-start(bf16[192,512]{1,0:T(8,128)(2,1)S(1)} %pad_maximum_fusion.8), channel_id=1, source_target_pairs={{0,8},{8,0},{16,24},{24,16},{1,9},{9,1},{17,25},{25,17},{2,10},{10... | collective-permute-start | bytes 589832 | tf_op jit(solution)/shard_map/ppermute | solution.py:174

commit v3 on v2

--- a/solution.py
+++ b/solution.py
@@ -41,45 +41,61 @@
     )(live_counts, route_index, activations)
 
 
-def product_kernel(count_j, count_k, place_ref, sel_ref, *refs):
-    pieces = refs[: count_j * count_k]
-    out_ref, weight, result, sems = refs[count_j * count_k :]
+def product_kernel(where, steps, started, place_ref, sel_ref, *refs):
+    refs = refs[1:] if started else refs
+    refs, (out_ref, weight, result, sems) = refs[:-4], refs[-4:]
     e, d = place_ref[0], place_ref[1]
-    half = pieces[0].shape[0] // 2
-    columns = pieces[0].shape[1]
+    _, hidden, columns = weight.shape
+    half = hidden // len(where) // 2
+    tall = result.shape[1] // 2
     copies = []
-    for k in range(count_k):
-        for j in range(count_j):
+    for n, k in enumerate(steps):
+        for j, places in enumerate(where):
+            ref, offset = refs[places[n][0]], places[n][1]
             for t in range(2):
-                row = pl.multiple_of((e ^ (2 * j + t)) * half, 16)
-                weight[k, pl.ds(row, half), :] = pieces[j * count_k + k][t * half : (t + 1) * half, :]
-        result[k] = jnp.dot(sel_ref[...], weight[k], preferred_element_type=f32).astype(bf16)
+                at = pl.multiple_of((e ^ (2 * j + t)) * half, 16)
+                weight[n, pl.ds(at, half), :] = ref[offset + t * half : offset + (t + 1) * half, :]
         at = pl.multiple_of((d ^ k) * columns, 128)
-        copy = pltpu.make_async_copy(result.at[k], out_ref.at[:, pl.ds(at, columns)], sems.at[k])
-        copy.start()
-        copies.append(copy)
+        for m in range(2):
+            part = slice(m * tall, (m + 1) * tall)
+            result[n, part] = jnp.dot(sel_ref[part, :], weight[n], preferred_element_type=f32).astype(bf16)
+            copy = pltpu.make_async_copy(
+                result.at[n, pl.ds(m * tall, tall), :],
+                out_ref.at[pl.ds(m * tall, tall), pl.ds(at, columns)],
+                sems.at[2 * n + m],
+            )
+            copy.start()
+            copies.append(copy)
     for copy in copies:
         copy.wait()
 
 
-def multiply(place, selected, pieces):
-    count_j, count_k = len(pieces), len(pieces[0])
+def multiply(place, selected, pieces, steps, total, begun=None):
+    arrays, where = [], []
+    for group in pieces:
+        where.append([])
+        for array, offset in group:
+            found = [n for n, other in enumerate(arrays) if other is array]
+            if not found:
+                arrays.append(array)
+            where[-1].append((found[0] if found else len(arrays) - 1, offset))
     rows, hidden = selected.shape
-    columns = pieces[0][0].shape[1]
-    flat = [v for group in pieces for v in group]
-    vmem = pl.BlockSpec(memory_space=pltpu.VMEM)
+    columns = arrays[0].shape[1]
+    vmem, anywhere = pl.BlockSpec(memory_space=pltpu.VMEM), pl.BlockSpec(memory_space=pl.ANY)
+    first = () if begun is None else (begun,)
     return pl.pallas_call(
-        functools.partial(product_kernel, count_j, count_k),
-        out_shape=jax.ShapeDtypeStruct((rows, columns * count_k), bf16),
-        in_specs=[pl.BlockSpec(memory_space=pltpu.SMEM), vmem] + [vmem] * len(flat),
-        out_specs=pl.BlockSpec(memory_space=pl.ANY),
+        functools.partial(product_kernel, where, steps, bool(first)),
+        out_shape=jax.ShapeDtypeStruct((rows, columns * total), bf16),
+        in_specs=[pl.BlockSpec(memory_space=pltpu.SMEM), vmem] + [anywhere] * len(first) + [vmem] * len(arrays),
+        out_specs=anywhere,
         scratch_shapes=[
-            pltpu.VMEM((count_k, hidden, columns), bf16),
-            pltpu.VMEM((count_k, rows, columns), bf16),
-            pltpu.SemaphoreType.DMA((count_k,)),
+            pltpu.VMEM((len(steps), hidden, columns), bf16),
+            pltpu.VMEM((len(steps), rows, columns), bf16),
+            pltpu.SemaphoreType.DMA((2 * len(steps),)),
         ],
+        input_output_aliases={2: 0} if first else {},
         compiler_params=pltpu.CompilerParams(vmem_limit_bytes=24 * 1024 * 1024),
-    )(place, selected, *flat)
+    )(place, selected, *first, *arrays)
 
 
 def step_kernel(place_ref, current_ref, next_ref, momentum_ref, master_ref, theirs_ref, *refs):
@@ -187,6 +203,7 @@
             out = out + v.astype(f32)
         return out.astype(bf16)
 
+    sel = select_rows(activations[0, 0], route_index[0, 0], live_counts)
     sx3 = blk((3,), (1, 3), grad)
     sy2 = blk((2,), (2, 3), grad)
     grad = after(grad, sx3, sy2)
@@ -198,18 +215,18 @@
     oy0, o0 = blk((0,), (1,), grad), blk((0,), (0,), grad)
     x3 = dperm(sx3, 1)
     y2 = dperm(sy2, 2)
+    y3 = dperm(after(add(ox3, x3[n2:]), sel), 2)
+    x2 = dperm(add(oy2, y2[n2:]), 1)
     x1 = dperm(sx1, 1)
-    y0 = dperm(sy0, 2)
-    y3 = dperm(add(ox3, x3[n2:]), 2)
-    x2 = dperm(add(oy2, y2[n2:]), 1)
+    y0 = dperm(after(sy0, y2), 2)
+    y1 = dperm(add(ox1, x1[n2:]), 2)
     t3 = add(o3, x3[:n2], y3)
     t2 = add(o2, y2[:n2], x2)
+    z2 = eperm(t2, 4)
     z3 = eperm(t3, 6)
-    z2 = eperm(t2, 4)
-    y1 = dperm(add(ox1, x1[n2:]), 2)
-    x0 = dperm(add(oy0, y0[n2:]), 1)
     t1 = add(o1, x1[:n2], y1)
     z1 = eperm(t1, 2)
+    x0 = dperm(add(oy0, y0[n2:]), 1)
     t0 = add(after(o0, z3, z2), y0[:n2], x0)
     recv = {0: t0, 1: z1, 2: z2, 3: z3}
     mom_t, mas_t = momentum.transpose(1, 0, 2), master_weights.transpose(1, 0, 2)
@@ -218,26 +235,27 @@
     got = eperm(other, 1)
     w = [jnp.concatenate([mine[j], got[j]], 0) for j in range(nj)]
     v = [w[0], None, None, None]
-    v[1] = eperm(w[1], 2)
     v[2] = eperm(w[2], 4)
     v[3] = eperm(w[3], 6)
-    full = [None] * 4
-    ax0 = dperm(v[0], 1)
-    by0 = dperm(v[1], 2)
-    ay0 = dperm(jnp.concatenate([v[0], ax0], 0), 2)
-    bx0 = dperm(jnp.concatenate([v[1], by0], 0), 1)
-    full[0] = [v[0], ax0, ay0[:n2], ay0[n2:]]
-    full[1] = [v[1], bx0[:n2], by0, bx0[n2:]]
-    ax1 = dperm(v[2], 1)
-    by1 = dperm(v[3], 2)
-    ay1 = dperm(jnp.concatenate([v[2], ax1], 0), 2)
-    bx1 = dperm(jnp.concatenate([v[3], by1], 0), 1)
-    full[2] = [v[2], ax1, ay1[:n2], ay1[n2:]]
-    full[3] = [v[3], bx1[:n2], by1, bx1[n2:]]
-    late = ay0
+    v[1] = eperm(w[1], 2)
+    ax = dperm(v[0], 1)
+    by = dperm(v[1], 2)
+    ay = dperm(jnp.concatenate([v[0], ax], 0), 2)
+    bx = dperm(jnp.concatenate([v[1], by], 0), 1)
+    cx = dperm(v[2], 1)
+    ey = dperm(v[3], 2)
+    cy = dperm(jnp.concatenate([v[2], cx], 0), 2)
+    ex = dperm(jnp.concatenate([v[3], ey], 0), 1)
+    pieces = [
+        [(v[0], 0), (ax, 0), (ay, 0), (ay, n2)],
+        [(v[1], 0), (bx, 0), (by, 0), (bx, n2)],
+        [(v[2], 0), (cx, 0), (cy, 0), (cy, n2)],
+        [(v[3], 0), (ex, 0), (ey, 0), (ex, n2)],
+    ]
+    late = ay
     new_mom = after(new_mom, late)
-    sel = select_rows(activations[0, 0], route_index[0, 0], live_counts)
-    out = multiply(place, sel, full)
+    begun = multiply(place, sel, [group[:1] for group in pieces], (0,), nd)
+    out = multiply(place, sel, [group[1:] for group in pieces], (1, 2, 3), nd, begun)
     return new_mom.transpose(1, 0, 2), out[None, None]
 
 

time: 60.1 us -> 58.2 us (0.968)
  waiting for transfers between devices: 19.4 us -> 15.4 us
  Pallas kernels: 5.78 us -> 7.14 us
  starting transfers between devices: 29.8 us -> 30.8 us
    ppermute x16, waiting for transfers between devices: 7.3 us -> 4.77 us  [dperm(): return lax.ppermute(v, 'dp', [(i, i ^ k) for i in range(nd)])]
    ppermute x8, waiting for transfers between devices: 12.1 us -> 10.6 us  [eperm(): return lax.ppermute(v, 'expert', [(i, i ^ q) for i in range(ne)])]
    pallas_call x1 -> x2, Pallas kernels: 2.68 us -> 4.05 us  [multiply(): pl.pallas_call(functools.partial(product_kernel, where, steps, bool(first...]
    ppermute x8, starting transfers between devices: 9.47 us -> 10.2 us  [eperm(): return lax.ppermute(v, 'expert', [(i, i ^ q) for i in range(ne)])]
  transfers between devices with their start and end apart: 24 -> 24, of which waited for: 13 -> 12; matrix products, arithmetic and copies ran while one was open for 3% -> 3% of each run, Pallas kernels for 3% -> 7%
where the time goes in v3:
time: 58.2 us; the launch traced here: 58.1 us
  starting transfers between devices  30.8 us (53%)
  waiting for transfers between devices  15.4 us (26%)
  Pallas kernels  7.14 us (12%)
  local copies, waits for them, and re-layouts  2.74 us (5%)
  between operations  1.55 us (3%)
    ppermute x16, starting transfers between devices, dperm(): return lax.ppermute(v, 'dp', [(i, i ^ k) for i in range(nd)])  20.5 us
    ppermute x8, waiting for transfers between devices, eperm(): return lax.ppermute(v, 'expert', [(i, i ^ q) for i in range(ne)])  10.6 us
    ppermute x8, starting transfers between devices, eperm(): return lax.ppermute(v, 'expert', [(i, i ^ q) for i in range(ne)])  10.2 us
    ppermute x16, waiting for transfers between devices, dperm(): return lax.ppermute(v, 'dp', [(i, i ^ k) for i in range(nd)])  4.77 us
    pallas_call x2, Pallas kernels, multiply(): pl.pallas_call(functools.partial(product_kernel, where, steps, bool(first...  4.05 us
    pallas_call x1, Pallas kernels, select_rows(): pl.pallas_call(select_kernel, out_shape=jax.ShapeDtypeStruct((rows, hidde...  2.06 us
    dynamic_slice x2, local copies, waits for them, and re-layouts, blk(): lax.dynamic_slice(g, ((e ^ 2 * j + t) * sr, (d ^ k) * cols), (sr, cols))  1.27 us
    unnamed x15, local copies, waits for them, and re-layouts  1.19 us
  transfers between devices with their start and end apart: 24, of which 12 were waited for; matrix products, arithmetic and copies ran while one was open for 3% of the time, Pallas kernels for 7%

profile of v3, /device:TPU:0, one launch (start us, length us, event | category | flops | bytes accessed | tf_op | source)
XLA Modules:
  0.0 58.1 jit_solution(17610635092863553561)
XLA Ops:
  0.7 1.1 %dynamic-slice_bitcast_fusion.3 = (bf16[48,512]{1,0:T(8,128)(2,1)S(1)}, bf16[48,512]{1,0:T(8,128)(2,1)S(1)}, bf16[48,512]{1,0:T(8,128)(2,1)S(1)}, bf16[48,512]{1...) fusion(bf16[1,1,384,2048]{3,2,1,0:T(8,128)(2,1)} %param.8, ...), kind=kLoop, calls=%fused_computation.39 | loop fusion | bytes 786460 | tf_op jit(solution)/shard_map/dynamic_slice | solution.py:197
  1.8 3.0 %collective-permute-start = (bf16[192,512]{1,0:T(8,128)(2,1)S(1)}, bf16[192,512]{1,0:T(8,128)(2,1)S(1)}, u32[]{:S(2)}, u32[]{:S(2)}) collective-permute-start(bf16[192,512]{1,0:T(8,128)(2,1)S(1)} %pad_maximum_fusion), channel_id=1, source_target_pairs={{0,8},{8,0},{16,24},{24,16},{1,9},{9,1},{17,25},{25,17},{2,10},{10... | collective-permute-start | bytes 589832 | tf_op jit(solution)/shard_map/ppermute | solution.py:190
  4.9 1.6 %collective-permute-start.3 = (bf16[192,512]{1,0:T(8,128)(2,1)S(1)}, bf16[192,512]{1,0:T(8,128)(2,1)S(1)}, u32[]{:S(2)}, u32[]{:S(2)}) collective-permute-start(bf16[192,512]{1,0:T(8,128)(2,1)S(1)} %pad_maximum_fusion.1), channel_id=1, source_target_pairs={{0,16},{8,24},{16,0},{24,8},{1,17},{9,25},{17,1},{25,9},{2,18},{10... | collective-permute-start | bytes 589832 | tf_op jit(solution)/shard_map/ppermute | solution.py:190
  6.4 0.2 fusion
  6.6 0.6 %collective-permute-start.8 = (bf16[192,512]{1,0:T(8,128)(2,1)S(1)}, bf16[192,512]{1,0:T(8,128)(2,1)S(1)}, u32[]{:S(2)}, u32[]{:S(2)}) collective-permute-start(bf16[192,512]{1,0:T(8,128)(2,1)S(1)} %pad_maximum_fusion.3), channel_id=1, source_target_pairs={{0,8},{8,0},{16,24},{24,16},{1,9},{9,1},{17,25},{25,17},{2,10},{10... | collective-permute-start | bytes 589832 | tf_op jit(solution)/shard_map/ppermute | solution.py:190
  7.9 0.1 copy.13.current_ref
  8.0 0.1 copy.14.next_ref
  8.1 2.1 %shard_map.95.sel_ref = bf16[512,384]{1,0:T(8,128)(2,1)} custom-call(s32[1,1]{1,0:T(1,128)S(6)} %copy.19.live_ref, s32[4,128]{1,0:T(4,128)} %bitcast.55, bf16[512,384]{1,0:T(8,128)(2,1)} %bitcast.54), custom_call_target="tpu_custom_call" | custom-call | tf_op jit(solution)/shard_map/pallas_call | solution.py:32
  10.1 0.1 pad_add_fusion.place_ref
  10.2 0.4 collective-permute-done
  10.6 2.2 %collective-permute-start.1 = (bf16[96,512]{1,0:T(8,128)(2,1)S(1)}, bf16[96,512]{1,0:T(8,128)(2,1)S(1)}, u32[]{:S(2)}, u32[]{:S(2)}) collective-permute-start(bf16[96,512]{1,0:T(8,128)(2,1)S(1)} %add_convert_fusion.7), channel_id=1, source_target_pairs={{0,16},{8,24},{16,0},{24,8},{1,17},{9,25},{17,1},{25,9},{2,18},{10... | collective-permute-start | bytes 294920 | tf_op jit(solution)/shard_map/ppermute | solution.py:190
  12.7 0.0 collective-permute-done.3
  12.8 1.6 %collective-permute-start.4 = (bf16[96,512]{1,0:T(8,128)(2,1)S(1)}, bf16[96,512]{1,0:T(8,128)(2,1)S(1)}, u32[]{:S(2)}, u32[]{:S(2)}) collective-permute-start(bf16[96,512]{1,0:T(8,128)(2,1)S(1)} %add_convert_fusion.5), channel_id=1, source_target_pairs={{0,8},{8,0},{16,24},{24,16},{1,9},{9,1},{17,25},{25,17},{2,10},{10... | collective-permute-start | bytes 294920 | tf_op jit(solution)/shard_map/ppermute | solution.py:190
  14.3 0.5 collective-permute-start.6
  14.8 0.0 collective-permute-done.8
  14.9 2.0 %collective-permute-start.9 = (bf16[96,512]{1,0:T(8,128)(2,1)S(1)}, bf16[96,512]{1,0:T(8,128)(2,1)S(1)}, u32[]{:S(2)}, u32[]{:S(2)}) collective-permute-start(bf16[96,512]{1,0:T(8,128)(2,1)S(1)} %add_convert_fusion.1), channel_id=1, source_target_pairs={{0,16},{8,24},{16,0},{24,8},{1,17},{9,25},{17,1},{25,9},{2,18},{10... | collective-permute-start | bytes 294920 | tf_op jit(solution)/shard_map/ppermute | solution.py:190
  16.9 3.7 %collective-permute-start.2 = (bf16[96,512]{1,0:T(8,128)(2,1)S(1)}, bf16[96,512]{1,0:T(8,128)(2,1)S(1)}, u32[]{:S(2)}, u32[]{:S(2)}) collective-permute-start(bf16[96,512]{1,0:T(8,128)(2,1)S(1)} %add_convert_fusion.6), channel_id=1, source_target_pairs={{0,6},{1,7},{2,4},{3,5},{4,2},{5,3},{6,0},{7,1},{8,14},{9,15},{10,... | collective-permute-start | bytes 294920 | tf_op jit(solution)/shard_map/ppermute | solution.py:193
  20.6 0.1 collective-permute-start.5
  20.7 0.9 %collective-permute-done.9 = bf16[96,512]{1,0:T(8,128)(2,1)S(1)} collective-permute-done((bf16[96,512]{1,0:T(8,128)(2,1)S(1)}, bf16[96,512]{1,0:T(8,128)(2,1)S(1)}, u32[]{:S(2)}, u32[]{:S(2)}) %collective-permute-start.9) | collective-permute-done | bytes 98336 | tf_op jit(solution)/shard_map/ppermute | solution.py:190
  21.6 1.6 %collective-permute-start.10 = (bf16[96,512]{1,0:T(8,128)(2,1)S(1)}, bf16[96,512]{1,0:T(8,128)(2,1)S(1)}, u32[]{:S(2)}, u32[]{:S(2)}) collective-permute-start(bf16[96,512]{1,0:T(8,128)(2,1)S(1)} %add_convert_fusion), channel_id=1, source_target_pairs={{0,2},{1,3},{2,0},{3,1},{4,6},{5,7},{6,4},{7,5},{8,10},{9,11},{10,... | collective-permute-start | bytes 294920 | tf_op jit(solution)/shard_map/ppermute | solution.py:193
  23.3 0.6 %collective-permute-start.7 = (bf16[96,512]{1,0:T(8,128)(2,1)S(1)}, bf16[96,512]{1,0:T(8,128)(2,1)S(1)}, u32[]{:S(2)}, u32[]{:S(2)}) collective-permute-start(bf16[96,512]{1,0:T(8,128)(2,1)S(1)} %add_convert_fusion.3), channel_id=1, source_target_pairs={{0,8},{8,0},{16,24},{24,16},{1,9},{9,1},{17,25},{25,17},{2,10},{10... | collective-permute-start | bytes 294920 | tf_op jit(solution)/shard_map/ppermute | solution.py:190
  23.9 3.0 %collective-permute-done.5.refs_2_ = bf16[96,512]{1,0:T(8,128)(2,1)S(1)} collective-permute-done((bf16[96,512]{1,0:T(8,128)(2,1)S(1)}, bf16[96,512]{1,0:T(8,128)(2,1)S(1)}, u32[]{:S(2)}, u32[]{:S(2)}) %collective-permute-start.5) | collective-permute-done | bytes 98336 | tf_op jit(solution)/shard_map/ppermute | solution.py:193
  26.9 0.5 collective-permute-done.10.refs_1_
  27.4 0.6 collective-permute-done.7
  28.1 0.1 collective-permute-start.11
  28.2 0.2 copy_bitcast_fusion
  28.4 1.2 %collective-permute-done.11.theirs_ref = bf16[4,48,512]{2,1,0:T(8,128)(2,1)S(1)} collective-permute-done((bf16[4,48,512]{2,1,0:T(8,128)(2,1)S(1)}, bf16[4,48,512]{2,1,0:T(8,128)(2,1)S(1)}, u32[]{:S(2)}, u32[]{:S(2)}) %collective-permute-start.11) | collective-permute-done | bytes 196640 | tf_op jit(solution)/shard_map/ppermute | solution.py:193
  29.6 1.0 %shard_map.96 = (f32[4,48,512]{2,1,0:T(8,128)S(1)}, bf16[4,48,512]{2,1,0:T(8,128)(2,1)S(1)}, bf16[4,48,512]{2,1,0:T(8,128)(2,1)S(1)}) custom-call(s32[2]{0:T(128)S(1)} %pad_add_fusion.place_ref, s32[8,1]{1,0:T(8,128)S(1)} %copy.13.current_ref, s32[8,1]{1,0:T(8,128)S(1)} %copy.14.next_ref, f32[4,48,512]{2,1,0:T(8,128)S(1)} %get-tuple-element.61.momentum_ref, ...), custom_call_target="tpu_custom_call" | custom-call | tf_op jit(solution)/shard_map/pallas_call | solution.py:134
  30.6 0.2 collective-permute-start.12
  30.8 1.3 %collective-permute-done.12 = bf16[4,48,512]{2,1,0:T(8,128)(2,1)S(1)} collective-permute-done((bf16[4,48,512]{2,1,0:T(8,128)(2,1)S(1)}, bf16[4,48,512]{2,1,0:T(8,128)(2,1)S(1)}, u32[]{:S(2)}, u32[]{:S(2)}) %collective-permute-start.12) | collective-permute-done | bytes 196640 | tf_op jit(solution)/shard_map/ppermute | solution.py:193
  32.2 0.6 %collective-permute-start.13 = (bf16[96,512]{1,0:T(8,128)(2,1)S(1)}, bf16[96,512]{1,0:T(8,128)(2,1)S(1)}, u32[]{:S(2)}, u32[]{:S(2)}) collective-permute-start(bf16[96,512]{1,0:T(8,128)(2,1)S(1)} %pad_maximum_fusion.10.refs_0_), channel_id=1, source_target_pairs={{0,8},{8,0},{16,24},{24,16},{1,9},{9,1},{17,25},{25,17},{2,10},{10... | collective-permute-start | bytes 294920 | tf_op jit(solution)/shard_map/ppermute | solution.py:190
  32.8 0.7 %collective-permute-start.15 = (bf16[96,512]{1,0:T(8,128)(2,1)S(1)}, bf16[96,512]{1,0:T(8,128)(2,1)S(1)}, u32[]{:S(2)}, u32[]{:S(2)}) collective-permute-start(bf16[96,512]{1,0:T(8,128)(2,1)S(1)} %pad_maximum_fusion.11), channel_id=1, source_target_pairs={{0,2},{1,3},{2,0},{3,1},{4,6},{5,7},{6,4},{7,5},{8,10},{9,11},{10,... | collective-permute-start | bytes 294920 | tf_op jit(solution)/shard_map/ppermute | solution.py:193
  33.4 3.2 %collective-permute-start.16 = (bf16[96,512]{1,0:T(8,128)(2,1)S(1)}, bf16[96,512]{1,0:T(8,128)(2,1)S(1)}, u32[]{:S(2)}, u32[]{:S(2)}) collective-permute-start(bf16[96,512]{1,0:T(8,128)(2,1)S(1)} %pad_maximum_fusion.12), channel_id=1, source_target_pairs={{0,4},{1,5},{2,6},{3,7},{4,0},{5,1},{6,2},{7,3},{8,12},{9,13},{10,... | collective-permute-start | bytes 294920 | tf_op jit(solution)/shard_map/ppermute | solution.py:193
  36.6 0.7 %collective-permute-start.17 = (bf16[96,512]{1,0:T(8,128)(2,1)S(1)}, bf16[96,512]{1,0:T(8,128)(2,1)S(1)}, u32[]{:S(2)}, u32[]{:S(2)}) collective-permute-start(bf16[96,512]{1,0:T(8,128)(2,1)S(1)} %pad_maximum_fusion.13), channel_id=1, source_target_pairs={{0,6},{1,7},{2,4},{3,5},{4,2},{5,3},{6,0},{7,1},{8,14},{9,15},{10,... | collective-permute-start | bytes 294920 | tf_op jit(solution)/shard_map/ppermute | solution.py:193
  37.3 1.6 %collective-permute-done.15.refs_1_ = bf16[96,512]{1,0:T(8,128)(2,1)S(1)} collective-permute-done((bf16[96,512]{1,0:T(8,128)(2,1)S(1)}, bf16[96,512]{1,0:T(8,128)(2,1)S(1)}, u32[]{:S(2)}, u32[]{:S(2)}) %collective-permute-start.15) | collective-permute-done | bytes 98336 | tf_op jit(solution)/shard_map/ppermute | solution.py:193
  38.9 1.2 %collective-permute-start.18 = (bf16[96,512]{1,0:T(8,128)(2,1)S(1)}, bf16[96,512]{1,0:T(8,128)(2,1)S(1)}, u32[]{:S(2)}, u32[]{:S(2)}) collective-permute-start(bf16[96,512]{1,0:T(8,128)(2,1)S(1)} %collective-permute-done.15.refs_1_), channel_id=1, source_target_pairs={{0,16},{8,24},{16,0},{24,8},{1,17},{9,25},{17,1},{25,9},{2,18},{10... | collective-permute-start | bytes 294920 | tf_op jit(solution)/shard_map/ppermute | solution.py:190
  40.1 0.9 %collective-permute-start.14 = (bf16[192,512]{1,0:T(8,128)(2,1)S(1)}, bf16[192,512]{1,0:T(8,128)(2,1)S(1)}, u32[]{:S(2)}, u32[]{:S(2)}) collective-permute-start(bf16[192,512]{1,0:T(8,128)(2,1)S(1)} %pad_maximum_fusion.5), channel_id=1, source_target_pairs={{0,16},{8,24},{16,0},{24,8},{1,17},{9,25},{17,1},{25,9},{2,18},{10... | collective-permute-start | bytes 589832 | tf_op jit(solution)/shard_map/ppermute | solution.py:190
  41.0 3.1 %collective-permute-done.16.refs_2_ = bf16[96,512]{1,0:T(8,128)(2,1)S(1)} collective-permute-done((bf16[96,512]{1,0:T(8,128)(2,1)S(1)}, bf16[96,512]{1,0:T(8,128)(2,1)S(1)}, u32[]{:S(2)}, u32[]{:S(2)}) %collective-permute-start.16) | collective-permute-done | bytes 98336 | tf_op jit(solution)/shard_map/ppermute | solution.py:193
  44.1 1.1 %collective-permute-start.22 = (bf16[96,512]{1,0:T(8,128)(2,1)S(1)}, bf16[96,512]{1,0:T(8,128)(2,1)S(1)}, u32[]{:S(2)}, u32[]{:S(2)}) collective-permute-start(bf16[96,512]{1,0:T(8,128)(2,1)S(1)} %collective-permute-done.17.refs_3_), channel_id=1, source_target_pairs={{0,16},{8,24},{16,0},{24,8},{1,17},{9,25},{17,1},{25,9},{2,18},{10... | collective-permute-start | bytes 294920 | tf_op jit(solution)/shard_map/ppermute | solution.py:190
  45.2 2.1 %collective-permute-start.19 = (bf16[192,512]{1,0:T(8,128)(2,1)S(1)}, bf16[192,512]{1,0:T(8,128)(2,1)S(1)}, u32[]{:S(2)}, u32[]{:S(2)}) collective-permute-start(bf16[192,512]{1,0:T(8,128)(2,1)S(1)} %pad_maximum_fusion.6), channel_id=1, source_target_pairs={{0,8},{8,0},{16,24},{24,16},{1,9},{9,1},{17,25},{25,17},{2,10},{10... | collective-permute-start | bytes 589832 | tf_op jit(solution)/shard_map/ppermute | solution.py:190
  47.3 1.7 %collective-permute-done.20.refs_5_ = bf16[96,512]{1,0:T(8,128)(2,1)S(1)} collective-permute-done((bf16[96,512]{1,0:T(8,128)(2,1)S(1)}, bf16[96,512]{1,0:T(8,128)(2,1)S(1)}, u32[]{:S(2)}, u32[]{:S(2)}) %collective-permute-start.20) | collective-permute-done | bytes 98336 | tf_op jit(solution)/shard_map/ppermute | solution.py:190
  49.1 0.9 %collective-permute-start.21 = (bf16[192,512]{1,0:T(8,128)(2,1)S(1)}, bf16[192,512]{1,0:T(8,128)(2,1)S(1)}, u32[]{:S(2)}, u32[]{:S(2)}) collective-permute-start(bf16[192,512]{1,0:T(8,128)(2,1)S(1)} %pad_maximum_fusion.7), channel_id=1, source_target_pairs={{0,16},{8,24},{16,0},{24,8},{1,17},{9,25},{17,1},{25,9},{2,18},{10... | collective-permute-start | bytes 589832 | tf_op jit(solution)/shard_map/ppermute | solution.py:190
  50.0 1.7 %collective-permute-start.23 = (bf16[192,512]{1,0:T(8,128)(2,1)S(1)}, bf16[192,512]{1,0:T(8,128)(2,1)S(1)}, u32[]{:S(2)}, u32[]{:S(2)}) collective-permute-start(bf16[192,512]{1,0:T(8,128)(2,1)S(1)} %pad_maximum_fusion.8), channel_id=1, source_target_pairs={{0,8},{8,0},{16,24},{24,16},{1,9},{9,1},{17,25},{25,17},{2,10},{10... | collective-permute-start | bytes 589832 | tf_op jit(solution)/shard_map/ppermute | solution.py:190
  51.8 1.7 %shard_map.97.refs_0_ = bf16[512,2048]{1,0:T(8,128)(2,1)} custom-call(s32[2]{0:T(128)S(1)} %pad_add_fusion.place_ref, bf16[512,384]{1,0:T(8,128)(2,1)S(1)} %copy-done, bf16[96,512]{1,0:T(8,128)(2,1)S(1)} %pad_maximum_fusion.10.refs_0_, bf16[96,512]{1,0:T(8,128)(2,1)S(1)} %collective-permute-done.15.refs_1_, ...), custom_call_target="tpu_custom_call" | custom-call | tf_op jit(solution)/shard_map/pallas_call | solution.py:86
  53.5 1.0 %copy.15 = f32[48,4,512]{2,1,0:T(4,128)} copy(f32[48,4,512]{2,0,1:T(8,128)S(1)} %bitcast.51) | data formatting | bytes 786432
  54.5 0.3 collective-permute-done.21.refs_6_
  54.8 1.0 %collective-permute-done.23.refs_7_ = bf16[192,512]{1,0:T(8,128)(2,1)S(1)} collective-permute-done((bf16[192,512]{1,0:T(8,128)(2,1)S(1)}, bf16[192,512]{1,0:T(8,128)(2,1)S(1)}, u32[]{:S(2)}, u32[]{:S(2)}) %collective-permute-start.23) | collective-permute-done | bytes 196640 | tf_op jit(solution)/shard_map/ppermute | solution.py:190
  55.7 2.3 %shard_map.98 = bf16[512,2048]{1,0:T(8,128)(2,1)} custom-call(s32[2]{0:T(128)S(1)} %pad_add_fusion.place_ref, bf16[512,384]{1,0:T(8,128)(2,1)S(1)} %copy-done, bf16[512,2048]{1,0:T(8,128)(2,1)} %shard_map.97.refs_0_, bf16[96,512]{1,0:T(8,128)(2,1)S(1)} %collective-permute-done.13.refs_1_, ...), custom_call_target="tpu_custom_call", output_to_operand_aliasing={{}: (2, {})} | custom-call | tf_op jit(solution)/shard_map/pallas_call | solution.py:86
  (51 shorter events, 0.5 us)
Async XLA Ops:
  0.6 5.8 %copy-start.1 = (bf16[1,1,384,2048]{3,2,1,0:T(8,128)(2,1)S(1)}, bf16[1,1,384,2048]{3,2,1,0:T(8,128)(2,1)}, u32[]{:S(2)}) copy-start(bf16[1,1,384,2048]{3,2,1,0:T(8,128)(2,1)} %param.8) | copy-start | bytes 4718596
  1.8 8.7 %collective-permute-start = (bf16[192,512]{1,0:T(8,128)(2,1)S(1)}, bf16[192,512]{1,0:T(8,128)(2,1)S(1)}, u32[]{:S(2)}, u32[]{:S(2)}) collective-permute-start(bf16[192,512]{1,0:T(8,128)(2,1)S(1)} %pad_maximum_fusion), channel_id=1, source_target_pairs={{0,8},{8,0},{16,24},{24,16},{1,9},{9,1},{17,25},{25,17},{2,10},{10... | collective-permute-start | bytes 589832 | tf_op jit(solution)/shard_map/ppermute | solution.py:190
  4.8 3.0 %copy-start.4 = (s32[8,1]{0,1:T(1,128)S(1)}, s32[8,1]{0,1:T(1,128)}, u32[]{:S(2)}) copy-start(s32[8,1]{0,1:T(1,128)} %param.11) | copy-start | bytes 100
  4.8 3.1 %copy-start.5 = (s32[8,1]{0,1:T(1,128)S(1)}, s32[8,1]{0,1:T(1,128)}, u32[]{:S(2)}) copy-start(s32[8,1]{0,1:T(1,128)} %param.12) | copy-start | bytes 100
  4.9 7.9 %collective-permute-start.3 = (bf16[192,512]{1,0:T(8,128)(2,1)S(1)}, bf16[192,512]{1,0:T(8,128)(2,1)S(1)}, u32[]{:S(2)}, u32[]{:S(2)}) collective-permute-start(bf16[192,512]{1,0:T(8,128)(2,1)S(1)} %pad_maximum_fusion.1), channel_id=1, source_target_pairs={{0,16},{8,24},{16,0},{24,8},{1,17},{9,25},{17,1},{25,9},{2,18},{10... | collective-permute-start | bytes 589832 | tf_op jit(solution)/shard_map/ppermute | solution.py:190
  6.6 8.2 %collective-permute-start.8 = (bf16[192,512]{1,0:T(8,128)(2,1)S(1)}, bf16[192,512]{1,0:T(8,128)(2,1)S(1)}, u32[]{:S(2)}, u32[]{:S(2)}) collective-permute-start(bf16[192,512]{1,0:T(8,128)(2,1)S(1)} %pad_maximum_fusion.3), channel_id=1, source_target_pairs={{0,8},{8,0},{16,24},{24,16},{1,9},{9,1},{17,25},{25,17},{2,10},{10... | collective-permute-start | bytes 589832 | tf_op jit(solution)/shard_map/ppermute | solution.py:190
  10.6 6.3 %collective-permute-start.1 = (bf16[96,512]{1,0:T(8,128)(2,1)S(1)}, bf16[96,512]{1,0:T(8,128)(2,1)S(1)}, u32[]{:S(2)}, u32[]{:S(2)}) collective-permute-start(bf16[96,512]{1,0:T(8,128)(2,1)S(1)} %add_convert_fusion.7), channel_id=1, source_target_pairs={{0,16},{8,24},{16,0},{24,8},{1,17},{9,25},{17,1},{25,9},{2,18},{10... | collective-permute-start | bytes 294920 | tf_op jit(solution)/shard_map/ppermute | solution.py:190
  12.8 15.4 %copy-start.2 = (f32[48,4,512]{2,1,0:T(4,128)S(1)}, f32[48,4,512]{2,1,0:T(4,128)}, u32[]{:S(2)}) copy-start(f32[48,4,512]{2,1,0:T(4,128)} %param.10) | copy-start | bytes 1179652
  12.8 15.4 %copy-start.3 = (f32[48,4,512]{2,1,0:T(4,128)S(1)}, f32[48,4,512]{2,1,0:T(4,128)}, u32[]{:S(2)}) copy-start(f32[48,4,512]{2,1,0:T(4,128)} %param.9) | copy-start | bytes 1179652
  12.8 7.8 %collective-permute-start.4 = (bf16[96,512]{1,0:T(8,128)(2,1)S(1)}, bf16[96,512]{1,0:T(8,128)(2,1)S(1)}, u32[]{:S(2)}, u32[]{:S(2)}) collective-permute-start(bf16[96,512]{1,0:T(8,128)(2,1)S(1)} %add_convert_fusion.5), channel_id=1, source_target_pairs={{0,8},{8,0},{16,24},{24,16},{1,9},{9,1},{17,25},{25,17},{2,10},{10... | collective-permute-start | bytes 294920 | tf_op jit(solution)/shard_map/ppermute | solution.py:190
  14.3 8.9 %collective-permute-start.6 = (bf16[192,512]{1,0:T(8,128)(2,1)S(1)}, bf16[192,512]{1,0:T(8,128)(2,1)S(1)}, u32[]{:S(2)}, u32[]{:S(2)}) collective-permute-start(bf16[192,512]{1,0:T(8,128)(2,1)S(1)} %pad_maximum_fusion.2), channel_id=1, source_target_pairs={{0,16},{8,24},{16,0},{24,8},{1,17},{9,25},{17,1},{25,9},{2,18},{10... | collective-permute-start | bytes 589832 | tf_op jit(solution)/shard_map/ppermute | solution.py:190
  14.9 6.7 %collective-permute-start.9 = (bf16[96,512]{1,0:T(8,128)(2,1)S(1)}, bf16[96,512]{1,0:T(8,128)(2,1)S(1)}, u32[]{:S(2)}, u32[]{:S(2)}) collective-permute-start(bf16[96,512]{1,0:T(8,128)(2,1)S(1)} %add_convert_fusion.1), channel_id=1, source_target_pairs={{0,16},{8,24},{16,0},{24,8},{1,17},{9,25},{17,1},{25,9},{2,18},{10... | collective-permute-start | bytes 294920 | tf_op jit(solution)/shard_map/ppermute | solution.py:190
  16.9 7.0 %collective-permute-start.2 = (bf16[96,512]{1,0:T(8,128)(2,1)S(1)}, bf16[96,512]{1,0:T(8,128)(2,1)S(1)}, u32[]{:S(2)}, u32[]{:S(2)}) collective-permute-start(bf16[96,512]{1,0:T(8,128)(2,1)S(1)} %add_convert_fusion.6), channel_id=1, source_target_pairs={{0,6},{1,7},{2,4},{3,5},{4,2},{5,3},{6,0},{7,1},{8,14},{9,15},{10,... | collective-permute-start | bytes 294920 | tf_op jit(solution)/shard_map/ppermute | solution.py:193
  20.6 6.3 %collective-permute-start.5 = (bf16[96,512]{1,0:T(8,128)(2,1)S(1)}, bf16[96,512]{1,0:T(8,128)(2,1)S(1)}, u32[]{:S(2)}, u32[]{:S(2)}) collective-permute-start(bf16[96,512]{1,0:T(8,128)(2,1)S(1)} %add_convert_fusion.4), channel_id=1, source_target_pairs={{0,4},{1,5},{2,6},{3,7},{4,0},{5,1},{6,2},{7,3},{8,12},{9,13},{10,... | collective-permute-start | bytes 294920 | tf_op jit(solution)/shard_map/ppermute | solution.py:193
  21.6 5.8 %collective-permute-start.10 = (bf16[96,512]{1,0:T(8,128)(2,1)S(1)}, bf16[96,512]{1,0:T(8,128)(2,1)S(1)}, u32[]{:S(2)}, u32[]{:S(2)}) collective-permute-start(bf16[96,512]{1,0:T(8,128)(2,1)S(1)} %add_convert_fusion), channel_id=1, source_target_pairs={{0,2},{1,3},{2,0},{3,1},{4,6},{5,7},{6,4},{7,5},{8,10},{9,11},{10,... | collective-permute-start | bytes 294920 | tf_op jit(solution)/shard_map/ppermute | solution.py:193
  23.3 4.7 %collective-permute-start.7 = (bf16[96,512]{1,0:T(8,128)(2,1)S(1)}, bf16[96,512]{1,0:T(8,128)(2,1)S(1)}, u32[]{:S(2)}, u32[]{:S(2)}) collective-permute-start(bf16[96,512]{1,0:T(8,128)(2,1)S(1)} %add_convert_fusion.3), channel_id=1, source_target_pairs={{0,8},{8,0},{16,24},{24,16},{1,9},{9,1},{17,25},{25,17},{2,10},{10... | collective-permute-start | bytes 294920 | tf_op jit(solution)/shard_map/ppermute | solution.py:190
  28.1 1.5 %collective-permute-start.11 = (bf16[4,48,512]{2,1,0:T(8,128)(2,1)S(1)}, bf16[4,48,512]{2,1,0:T(8,128)(2,1)S(1)}, u32[]{:S(2)}, u32[]{:S(2)}) collective-permute-start(bf16[4,48,512]{2,1,0:T(8,128)(2,1)S(1)} %pad_maximum_fusion.4), channel_id=1, source_target_pairs={{0,1},{1,0},{2,3},{3,2},{4,5},{5,4},{6,7},{7,6},{8,9},{9,8},{10,11... | collective-permute-start | bytes 589832 | tf_op jit(solution)/shard_map/ppermute | solution.py:193
  30.6 1.5 %collective-permute-start.12 = (bf16[4,48,512]{2,1,0:T(8,128)(2,1)S(1)}, bf16[4,48,512]{2,1,0:T(8,128)(2,1)S(1)}, u32[]{:S(2)}, u32[]{:S(2)}) collective-permute-start(bf16[4,48,512]{2,1,0:T(8,128)(2,1)S(1)} %get-tuple-element.16), channel_id=1, source_target_pairs={{0,1},{1,0},{2,3},{3,2},{4,5},{5,4},{6,7},{7,6},{8,9},{9,8},{10,11... | collective-permute-start | bytes 589832 | tf_op jit(solution)/shard_map/ppermute | solution.py:193
  30.8 20.9 %copy-start = (bf16[512,384]{1,0:T(8,128)(2,1)S(1)}, bf16[512,384]{1,0:T(8,128)(2,1)}, u32[]{:S(2)}) copy-start(bf16[512,384]{1,0:T(8,128)(2,1)} %shard_map.95.sel_ref) | copy-start | bytes 1179652
  32.2 8.0 %collective-permute-start.13 = (bf16[96,512]{1,0:T(8,128)(2,1)S(1)}, bf16[96,512]{1,0:T(8,128)(2,1)S(1)}, u32[]{:S(2)}, u32[]{:S(2)}) collective-permute-start(bf16[96,512]{1,0:T(8,128)(2,1)S(1)} %pad_maximum_fusion.10.refs_0_), channel_id=1, source_target_pairs={{0,8},{8,0},{16,24},{24,16},{1,9},{9,1},{17,25},{25,17},{2,10},{10... | collective-permute-start | bytes 294920 | tf_op jit(solution)/shard_map/ppermute | solution.py:190
  32.8 6.2 %collective-permute-start.15 = (bf16[96,512]{1,0:T(8,128)(2,1)S(1)}, bf16[96,512]{1,0:T(8,128)(2,1)S(1)}, u32[]{:S(2)}, u32[]{:S(2)}) collective-permute-start(bf16[96,512]{1,0:T(8,128)(2,1)S(1)} %pad_maximum_fusion.11), channel_id=1, source_target_pairs={{0,2},{1,3},{2,0},{3,1},{4,6},{5,7},{6,4},{7,5},{8,10},{9,11},{10,... | collective-permute-start | bytes 294920 | tf_op jit(solution)/shard_map/ppermute | solution.py:193
  33.4 10.7 %collective-permute-start.16 = (bf16[96,512]{1,0:T(8,128)(2,1)S(1)}, bf16[96,512]{1,0:T(8,128)(2,1)S(1)}, u32[]{:S(2)}, u32[]{:S(2)}) collective-permute-start(bf16[96,512]{1,0:T(8,128)(2,1)S(1)} %pad_maximum_fusion.12), channel_id=1, source_target_pairs={{0,4},{1,5},{2,6},{3,7},{4,0},{5,1},{6,2},{7,3},{8,12},{9,13},{10,... | collective-permute-start | bytes 294920 | tf_op jit(solution)/shard_map/ppermute | solution.py:193
  36.6 7.5 %collective-permute-start.17 = (bf16[96,512]{1,0:T(8,128)(2,1)S(1)}, bf16[96,512]{1,0:T(8,128)(2,1)S(1)}, u32[]{:S(2)}, u32[]{:S(2)}) collective-permute-start(bf16[96,512]{1,0:T(8,128)(2,1)S(1)} %pad_maximum_fusion.13), channel_id=1, source_target_pairs={{0,6},{1,7},{2,4},{3,5},{4,2},{5,3},{6,0},{7,1},{8,14},{9,15},{10,... | collective-permute-start | bytes 294920 | tf_op jit(solution)/shard_map/ppermute | solution.py:193
  38.9 6.3 %collective-permute-start.18 = (bf16[96,512]{1,0:T(8,128)(2,1)S(1)}, bf16[96,512]{1,0:T(8,128)(2,1)S(1)}, u32[]{:S(2)}, u32[]{:S(2)}) collective-permute-start(bf16[96,512]{1,0:T(8,128)(2,1)S(1)} %collective-permute-done.15.refs_1_), channel_id=1, source_target_pairs={{0,16},{8,24},{16,0},{24,8},{1,17},{9,25},{17,1},{25,9},{2,18},{10... | collective-permute-start | bytes 294920 | tf_op jit(solution)/shard_map/ppermute | solution.py:190
  40.1 13.4 %collective-permute-start.14 = (bf16[192,512]{1,0:T(8,128)(2,1)S(1)}, bf16[192,512]{1,0:T(8,128)(2,1)S(1)}, u32[]{:S(2)}, u32[]{:S(2)}) collective-permute-start(bf16[192,512]{1,0:T(8,128)(2,1)S(1)} %pad_maximum_fusion.5), channel_id=1, source_target_pairs={{0,16},{8,24},{16,0},{24,8},{1,17},{9,25},{17,1},{25,9},{2,18},{10... | collective-permute-start | bytes 589832 | tf_op jit(solution)/shard_map/ppermute | solution.py:190
  44.1 4.9 %collective-permute-start.20 = (bf16[96,512]{1,0:T(8,128)(2,1)S(1)}, bf16[96,512]{1,0:T(8,128)(2,1)S(1)}, u32[]{:S(2)}, u32[]{:S(2)}) collective-permute-start(bf16[96,512]{1,0:T(8,128)(2,1)S(1)} %collective-permute-done.16.refs_2_), channel_id=1, source_target_pairs={{0,8},{8,0},{16,24},{24,16},{1,9},{9,1},{17,25},{25,17},{2,10},{10... | collective-permute-start | bytes 294920 | tf_op jit(solution)/shard_map/ppermute | solution.py:190
  44.1 5.9 %collective-permute-start.22 = (bf16[96,512]{1,0:T(8,128)(2,1)S(1)}, bf16[96,512]{1,0:T(8,128)(2,1)S(1)}, u32[]{:S(2)}, u32[]{:S(2)}) collective-permute-start(bf16[96,512]{1,0:T(8,128)(2,1)S(1)} %collective-permute-done.17.refs_3_), channel_id=1, source_target_pairs={{0,16},{8,24},{16,0},{24,8},{1,17},{9,25},{17,1},{25,9},{2,18},{10... | collective-permute-start | bytes 294920 | tf_op jit(solution)/shard_map/ppermute | solution.py:190
  45.2 9.3 %collective-permute-start.19 = (bf16[192,512]{1,0:T(8,128)(2,1)S(1)}, bf16[192,512]{1,0:T(8,128)(2,1)S(1)}, u32[]{:S(2)}, u32[]{:S(2)}) collective-permute-start(bf16[192,512]{1,0:T(8,128)(2,1)S(1)} %pad_maximum_fusion.6), channel_id=1, source_target_pairs={{0,8},{8,0},{16,24},{24,16},{1,9},{9,1},{17,25},{25,17},{2,10},{10... | collective-permute-start | bytes 589832 | tf_op jit(solution)/shard_map/ppermute | solution.py:190
  49.1 5.7 %collective-permute-start.21 = (bf16[192,512]{1,0:T(8,128)(2,1)S(1)}, bf16[192,512]{1,0:T(8,128)(2,1)S(1)}, u32[]{:S(2)}, u32[]{:S(2)}) collective-permute-start(bf16[192,512]{1,0:T(8,128)(2,1)S(1)} %pad_maximum_fusion.7), channel_id=1, source_target_pairs={{0,16},{8,24},{16,0},{24,8},{1,17},{9,25},{17,1},{25,9},{2,18},{10... | collective-permute-start | bytes 589832 | tf_op jit(solution)/shard_map/ppermute | solution.py:190
  50.0 5.7 %collective-permute-start.23 = (bf16[192,512]{1,0:T(8,128)(2,1)S(1)}, bf16[192,512]{1,0:T(8,128)(2,1)S(1)}, u32[]{:S(2)}, u32[]{:S(2)}) collective-permute-start(bf16[192,512]{1,0:T(8,128)(2,1)S(1)} %pad_maximum_fusion.8), channel_id=1, source_target_pairs={{0,8},{8,0},{16,24},{24,16},{1,9},{9,1},{17,25},{25,17},{2,10},{10... | collective-permute-start | bytes 589832 | tf_op jit(solution)/shard_map/ppermute | solution.py:190
